TPU v7x, 512 devices: a whole 4x8x8 slice. The times are simulated.
512 devices in a mesh: req: 32 (over z, x), seq: 16 (over y, core).
Axes of the slice: x: 4, y: 8, z: 8, core: 2. Of those that a mesh axis runs over, the one named last changes fastest.
Arguments:
- transformer_tokens: bfloat16 [32, 96, 16, 64], P('req', None, 'seq'), may hold values from -6 to 6
- frames: int32 [32], replicated, may hold values from 1 to 96, as said below
- heights: int32 [32], replicated, may hold values from 4 to 8
- widths: int32 [32], replicated, may hold values from 4 to 8
- tile_decode_device: int32 [32, 16, 3], replicated, may hold values from -1 to 31, as said below
- tile_device_slot: int32 [32, 16, 3], replicated, may hold values from -1 to 1, as said below
- stem_conv_weight: bfloat16 [3, 3, 3, 16, 256], replicated, may hold values from -0.3125 to 0.3125
- stem_conv_bias: float32 [256], replicated, may hold values from -3 to 3
- upsample_first_weight: bfloat16 [3, 3, 3, 256, 256], replicated, may hold values from -0.078125 to 0.078125
- upsample_first_bias: float32 [256], replicated, may hold values from -3 to 3
- upsample_second_weight: bfloat16 [3, 3, 3, 256, 256], replicated, may hold values from -0.078125 to 0.078125
- upsample_second_bias: float32 [256], replicated, may hold values from -3 to 3
Outputs:
- decoded: bfloat16 [32, 16, 2, 2, 16, 16, 256], P('req', 'seq')
Inputs may be any that keep to these rules, and one draw needn't show every extreme that they name: Request r has frames[r] latent frames, the rest of its 96 are padding. Of the two requests r and r + 16 exactly one has 96 frames; the other has at most 32. `tile_decode_device`: -1 exactly for tiles whose first frame is at or past the request's frame count; otherwise r or (r + 16) mod 32 for a tile of request r. `tile_device_slot`: -1 exactly where tile_decode_device is -1; no two tiles of a column share device and slot; in every frame column the request with 96 frames keeps exactly two of its three tiles on its own device and hands exactly one to its paired device, so that device is full in every column.
All inputs are finite; a program needn't handle non-finite values.
Results may differ from a plain program's by a relative error of at most 0.0043.
Values may be sent and summed in bfloat16 or wider, within the bound.
No kernel may reach another device: no remote copies, remote signals or barrier semaphores. Data moves between devices by JAX's collectives and lax.ppermute only.
A program may use at most 64 MiB of HBM per device.

v0:
```python
import jax
import jax.numpy as jnp
from jax import lax
from jax.sharding import PartitionSpec as P

LAT_C = 16
LAT_H = 8
LAT_W = 8
TF = 2
CAP = 2


def passed_along(value, axis, by):
    peers = lax.axis_size(axis)
    return lax.ppermute(value, axis, [(i, (i + by) % peers) for i in range(peers)])


def unpatchify(tokens):
    lead = tokens.shape[:-2]
    half_rows = LAT_H // 2
    half_cols = LAT_W // 2
    shaped = tokens.reshape(lead + (half_rows, half_cols, LAT_C, 2, 2))
    count = len(lead)
    order = tuple(range(count)) + (count, count + 3, count + 1, count + 4, count + 2)
    return jnp.transpose(shaped, order).reshape(lead + (LAT_H, LAT_W, LAT_C))


def causal_conv(inputs, weight, biases):
    batch_size, frame_total, row_total, col_total, in_chans = inputs.shape
    out_frames = frame_total - 2
    padded = jnp.pad(inputs, ((0, 0), (0, 0), (1, 1), (1, 1), (0, 0)))
    kernel = weight.reshape(3, 3, 3 * in_chans, weight.shape[-1])
    summed = jnp.zeros(
        (batch_size * out_frames * row_total * col_total, weight.shape[-1]), jnp.float32
    )
    for row_tap in range(3):
        for col_tap in range(3):
            window = padded[:, :, row_tap : row_tap + row_total, col_tap : col_tap + col_total, :]
            stacked = jnp.concatenate(
                [window[:, time_tap : time_tap + out_frames] for time_tap in range(3)], axis=-1
            )
            summed = summed + jnp.dot(
                stacked.reshape(-1, 3 * in_chans),
                kernel[row_tap, col_tap],
                preferred_element_type=jnp.float32,
            )
    return summed.reshape(batch_size, out_frames, row_total, col_total, -1) + biases


def region(frame_ok, scale, row_limit, col_limit, row_total, col_total):
    row_ok = jnp.arange(row_total, dtype=jnp.int32)[None, :] < (scale * row_limit)[:, None]
    col_ok = jnp.arange(col_total, dtype=jnp.int32)[None, :] < (scale * col_limit)[:, None]
    allowed = frame_ok[:, :, None, None] & row_ok[:, None, :, None] & col_ok[:, None, None, :]
    return allowed[..., None]


def stem(latent, window_start, frame_count, row_limit, col_limit, weight, biases):
    window = latent.shape[1]
    row_total = latent.shape[2]
    col_total = latent.shape[3]
    frame_at = window_start[:, None] + jnp.arange(window, dtype=jnp.int32)[None, :]
    started = frame_at >= 0
    visible = started & (frame_at < frame_count[:, None])
    inputs = jnp.where(
        region(visible, 1, row_limit, col_limit, row_total, col_total),
        latent,
        jnp.zeros((), latent.dtype),
    )
    hidden = jax.nn.silu(causal_conv(inputs, weight, biases))
    return jnp.where(
        region(started[:, 2:], 1, row_limit, col_limit, row_total, col_total), hidden, 0.0
    ).astype(jnp.bfloat16)


def upper(
    hidden_one,
    first_frame,
    frame_count,
    row_limit,
    col_limit,
    is_live,
    upsample_first_weight,
    upsample_first_bias,
    upsample_second_weight,
    upsample_second_bias,
):
    window = hidden_one.shape[1]
    row_total = hidden_one.shape[2]
    col_total = hidden_one.shape[3]
    frame_at = first_frame[:, None] + jnp.arange(window, dtype=jnp.int32)[None, :]
    started = frame_at >= 0
    finished = (frame_at < frame_count[:, None]) & is_live[:, None]
    hidden_two = jax.nn.silu(causal_conv(hidden_one, upsample_first_weight, upsample_first_bias))
    hidden_two = jnp.where(
        region(started[:, 2:], 1, row_limit, col_limit, row_total, col_total), hidden_two, 0.0
    ).astype(jnp.bfloat16)
    upsampled = jnp.repeat(jnp.repeat(hidden_two, 2, axis=2), 2, axis=3)
    result = jax.nn.silu(causal_conv(upsampled, upsample_second_weight, upsample_second_bias))
    result = jnp.where(
        region(finished[:, 4:], 2, row_limit, col_limit, 2 * row_total, 2 * col_total), result, 0.0
    )
    return result.astype(jnp.bfloat16)


def lower_rows(shifted, back_step, my_column):
    widths_pad = ((1, 0),) + ((0, 0),) * (shifted.ndim - 1)
    lowered = jnp.pad(shifted, widths_pad)[:-1]
    return jnp.where(my_column >= back_step, shifted, lowered)


def body(
    transformer_tokens,
    frames,
    heights,
    widths,
    tile_decode_device,
    tile_device_slot,
    stem_conv_weight,
    stem_conv_bias,
    upsample_first_weight,
    upsample_first_bias,
    upsample_second_weight,
    upsample_second_bias,
):
    seq_count = lax.axis_size("seq")
    req_count = lax.axis_size("req")
    my_column = lax.axis_index("seq")
    my_request = lax.axis_index("req")
    local_tokens = transformer_tokens[0]
    frame_total, patch_part, patch_chans = local_tokens.shape
    tiles_per = frame_total // (seq_count * TF)
    row_ids = jnp.arange(tiles_per, dtype=jnp.int32)
    own_tiles = row_ids * seq_count + my_column
    own_count = jnp.full((tiles_per,), frames[my_request], jnp.int32)
    own_rows = jnp.full((tiles_per,), heights[my_request], jnp.int32)
    own_cols = jnp.full((tiles_per,), widths[my_request], jnp.int32)
    column_tiles = lax.all_to_all(
        local_tokens.reshape(tiles_per, seq_count, TF, patch_part, patch_chans),
        "seq",
        split_axis=1,
        concat_axis=3,
        tiled=True,
    )[:, 0]
    latent_back = (TF + 1) // TF
    pieces = []
    back_step = 1
    shifted = passed_along(column_tiles, "seq", back_step)
    pieces.append(lower_rows(shifted, back_step, my_column))
    pieces.append(column_tiles)
    latent = unpatchify(jnp.concatenate(pieces, axis=1))
    own_hidden = stem(
        latent, own_tiles * TF - 2, own_count, own_rows, own_cols, stem_conv_weight, stem_conv_bias
    )
    hidden_back = (TF + 3) // TF
    pieces = []
    for back_step in range(hidden_back, 0, -1):
        shifted = passed_along(own_hidden, "seq", back_step)
        pieces.append(lower_rows(shifted, back_step, my_column))
    pieces.append(own_hidden)
    hidden_one = jnp.concatenate(pieces, axis=1)
    half = req_count // 2
    partner = (my_request + half) % req_count
    places = jnp.arange(CAP, dtype=jnp.int32)
    own_device = tile_decode_device[my_request, my_column]
    own_slot = tile_device_slot[my_request, my_column]
    flat_hidden = hidden_one.reshape(tiles_per, -1)
    outgoing = ((own_device == partner)[None, :] & (own_slot[None, :] == places[:, None])).astype(
        jnp.bfloat16
    )
    buffer = jnp.dot(outgoing, flat_hidden, preferred_element_type=jnp.float32).astype(jnp.bfloat16)
    received = passed_along(buffer, "req", half)
    kept = (own_device == my_request)[None, :] & (own_slot[None, :] == places[:, None])
    partner_device = tile_decode_device[partner, my_column]
    partner_slot = tile_device_slot[partner, my_column]
    incoming = (partner_device == my_request)[None, :] & (partner_slot[None, :] == places[:, None])
    from_partner = jnp.any(incoming, axis=1)
    is_live = jnp.any(kept, axis=1) | from_partner
    local_rows = jnp.dot(
        kept.astype(jnp.bfloat16), flat_hidden, preferred_element_type=jnp.float32
    ).astype(jnp.bfloat16)
    slot_hidden = jnp.where(from_partner[:, None], received, local_rows)
    row_index = jnp.sum(jnp.where(kept, row_ids[None, :], 0), axis=1) + jnp.sum(
        jnp.where(incoming, row_ids[None, :], 0), axis=1
    )
    tile_index = row_index * seq_count + my_column
    first_frame = tile_index * TF - 4
    frame_count = jnp.where(from_partner, frames[partner], frames[my_request])
    row_limit = jnp.where(from_partner, heights[partner], heights[my_request])
    col_limit = jnp.where(from_partner, widths[partner], widths[my_request])
    shaped = slot_hidden.reshape((CAP,) + hidden_one.shape[1:])
    decoded = upper(
        shaped,
        first_frame,
        frame_count,
        row_limit,
        col_limit,
        is_live,
        upsample_first_weight,
        upsample_first_bias,
        upsample_second_weight,
        upsample_second_bias,
    )
    return decoded[None, None]


def solution(mesh):
    placed = (P("req", None, "seq", None), P(), P(), P(), P(), P(), P(), P(), P(), P(), P(), P())
    return jax.shard_map(
        body,
        mesh=mesh,
        in_specs=placed,
        out_specs=P("req", "seq", None, None, None, None, None),
        check_vma=False,
    )
```

profile of v0, /device:TPU:68, one launch (start us, length us, event | category | flops | bytes accessed | tf_op | source)
XLA Modules:
  0.0 93.2 jit_solution(1454342260751489799)
XLA Ops:
  0.0 0.8 copy.27
  0.8 0.7 reshape.402
  1.5 7.2 %all-to-all-start = ((bf16[16,2,192]{2,1,0:T(2,128)(2,1)}), bf16[16,2,192]{2,1,0:T(2,128)(2,1)S(1)}, u32[]{:S(2)}, u32[]{:S(2)}) async-start(bf16[16,2,192]{2,1,0:T(2,128)(2,1)} %reshape.402), calls=%async_computation | async-start | bytes 32768 | tf_op jit(solution)/shard_map/all_to_all | solution.py:137
  8.8 1.4 %fusion.17 = (s32[1]{0:T(128)}, s32[1]{0:T(128)}, s32[1]{0:T(128)}, s32[1]{0:T(128)}) fusion(s32[32]{0:T(128)} %param.13, s32[]{:T(128)S(6)} %select_n.118, s32[]{:T(128)S(6)} %select_n.114, s32[32]{0:T(128)} %param.14), kind=kLoop, calls=%fused_computation.212 | loop fusion | bytes 40 | tf_op jit(solution)/shard_map/dynamic_slice | solution.py:187
  10.2 0.6 iota_compare_fusion.1
  10.8 1.4 %fusion.19 = (s32[1]{0:T(128)}, s32[1]{0:T(128)}) fusion(s32[32]{0:T(128)} %param.15, s32[]{:T(128)S(6)} %select_n.118, s32[]{:T(128)S(6)} %select_n.114), kind=kLoop, calls=%fused_computation.214 | loop fusion | bytes 24 | tf_op jit(solution)/shard_map/dynamic_slice | solution.py:189
  12.2 0.6 iota_compare_fusion
  12.8 0.7 fusion.7
  13.9 1.1 %compare_reduce_fusion.1 = (pred[3]{0:T(512)(128)(4,1)S(1)}, pred[3]{0:T(512)(128)(4,1)S(1)}, pred[3]{0:T(512)(128)(4,1)S(1)}) fusion(s32[32,16,3]{0,1,2:T(8,128)} %param.16, s32[]{:T(128)S(6)} %select_n.118, s32[]{:T(128)S(6)} %select_n.115, s32[]{:T(128)S(6)} %axis_index.23, s32[]{:T(128)S(6)} %select_n.117, s32[]{:T(128)S(6)} %select_n.114), kind=kLoop, calls=%fused_computation.173 | loop fusion | flops 9 | bytes 53 | tf_op jit(solution)/shard_map/eq | solution.py:175
  15.0 1.1 %dynamic-slice_reduce_fusion = (s32[3]{0:T(128)S(1)}, s32[3]{0:T(128)S(1)}) fusion(s32[32,16,3]{0,1,2:T(8,128)} %param.17, s32[]{:T(128)S(6)} %select_n.118, s32[]{:T(128)S(6)} %select_n.115, s32[]{:T(128)S(6)} %select_n.114), kind=kLoop, calls=%fused_computation.188 | loop fusion | bytes 60 | tf_op jit(solution)/shard_map/dynamic_slice | solution.py:174
  16.5 3.7 %broadcast_multiply_fusion.1 = (s32[2]{0:T(128)S(1)}, s32[2]{0:T(128)S(1)}, s32[2]{0:T(128)S(1)}, s32[2]{0:T(128)S(1)}, s32[2]{0:T(128)S(1)}) fusion(pred[2]{0:T(512)(128)(4,1)S(1)} %get-tuple-element.113, s32[]{:T(128)} %bitcast.3, s32[]{:T(128)} %bitcast.2, s32[]{:T(128)} %bitcast.1, s32[]{:T(128)} %bitcast, s32[]{:T(128)} %bitcast.5, s32[]{:T(128)} %bitcast.4), kind=kLoop, calls=%fused_computation.210 | loop fusion | flops 10 | bytes 66 | tf_op jit(solution)/shard_map/mul | solution.py:51
  21.0 0.4 collective-permute-start
  21.7 0.7 copy.32
  22.4 3.1 %collective-permute-done = bf16[3,2,16,64]{3,1,0,2:T(2,128)(2,1)S(1)} collective-permute-done((bf16[3,2,16,64]{3,1,0,2:T(2,128)(2,1)S(1)}, bf16[3,2,16,64]{3,1,0,2:T(2,128)(2,1)S(1)}, u32[]{:S(2)}, u32[]{:S(2)}) %collective-permute-start) | collective-permute-done | bytes 12320 | tf_op jit(solution)/shard_map/ppermute | solution.py:15
  25.8 0.7 copy.31
  27.0 0.5 pad_slice_fusion.50
  31.0 2.6 %collective-permute-start.1 = (bf16[3,2,8,8,256]{4,3,2,1,0:T(8,128)(2,1)S(1)}, bf16[3,2,8,8,256]{4,3,2,1,0:T(8,128)(2,1)S(1)}, u32[]{:S(2)}, u32[]{:S(2)}) collective-permute-start(bf16[3,2,8,8,256]{4,3,2,1,0:T(8,128)(2,1)S(1)} %select_convert_fusion.2), channel_id=1, source_target_pairs={{0,2},{1,3},{2,4},{3,5},{4,6},{5,7},{6,8},{7,9},{8,10},{9,11},{10,... | collective-permute-start | bytes 589832 | tf_op jit(solution)/shard_map/ppermute | solution.py:15
  33.5 3.6 %collective-permute-done.2 = bf16[3,2,8,8,256]{4,3,2,1,0:T(8,128)(2,1)S(1)} collective-permute-done((bf16[3,2,8,8,256]{4,3,2,1,0:T(8,128)(2,1)S(1)}, bf16[3,2,8,8,256]{4,3,2,1,0:T(8,128)(2,1)S(1)}, u32[]{:S(2)}, u32[]{:S(2)}) %collective-permute-start.2) | collective-permute-done | bytes 196640 | tf_op jit(solution)/shard_map/ppermute | solution.py:15
  37.2 4.5 %collective-permute-done.1 = bf16[3,2,8,8,256]{4,3,2,1,0:T(8,128)(2,1)S(1)} collective-permute-done((bf16[3,2,8,8,256]{4,3,2,1,0:T(8,128)(2,1)S(1)}, bf16[3,2,8,8,256]{4,3,2,1,0:T(8,128)(2,1)S(1)}, u32[]{:S(2)}, u32[]{:S(2)}) %collective-permute-start.1) | collective-permute-done | bytes 196640 | tf_op jit(solution)/shard_map/ppermute | solution.py:15
  41.7 0.5 copy.34
  42.3 0.6 convolution_convert_fusion.1
  42.8 10.2 %collective-permute-start.3 = (bf16[2,98304]{1,0:T(2,128)(2,1)S(1)}, bf16[2,98304]{1,0:T(2,128)(2,1)S(1)}, u32[]{:S(2)}, u32[]{:S(2)}) collective-permute-start(bf16[2,98304]{1,0:T(2,128)(2,1)S(1)} %convolution_convert_fusion.1), channel_id=1, source_target_pairs={{0,256},{16,272},{32,288},{48,304},{64,320},{80,336},{96,352},{112... | collective-permute-start | bytes 1179656 | tf_op jit(solution)/shard_map/ppermute | solution.py:15
  53.2 17.6 %collective-permute-done.3 = bf16[2,98304]{1,0:T(2,128)(2,1)S(1)} collective-permute-done((bf16[2,98304]{1,0:T(2,128)(2,1)S(1)}, bf16[2,98304]{1,0:T(2,128)(2,1)S(1)}, u32[]{:S(2)}, u32[]{:S(2)}) %collective-permute-start.3) | collective-permute-done | bytes 393248 | tf_op jit(solution)/shard_map/ppermute | solution.py:15
  70.8 0.7 fusion
  71.6 0.8 pad_slice_fusion.26
  72.7 1.7 %copy-done = bf16[3,3,3,256,256]{4,3,2,1,0:T(8,128)(2,1)S(1)} copy-done((bf16[3,3,3,256,256]{4,3,2,1,0:T(8,128)(2,1)S(1)}, bf16[3,3,3,256,256]{4,3,2,1,0:T(8,128)(2,1)}, u32[]{:S(2)}) %copy-start) | copy-done | bytes 3538968
  74.9 0.4 convolution_add_fusion.15
  75.3 0.4 convolution_add_fusion.14
  75.8 0.4 convolution_add_fusion.13
  76.2 0.4 convolution_add_fusion.12
  77.1 0.4 convolution_add_fusion.10
  77.5 0.4 convolution_add_fusion.9
  78.0 0.4 convolution_add_fusion.8
  78.8 0.9 broadcast_in_dim.171
  79.7 0.7 reshape.385
  80.4 3.4 %pad_slice_fusion.2 = (bf16[2,2,16,16,256]{4,3,2,1,0:T(8,128)(2,1)S(1)}, bf16[2,2,16,16,256]{4,3,2,1,0:T(8,128)(2,1)S(1)}, bf16[2,2,16,16,256]{4,3,2,1,0:T(8,128...) fusion(bf16[2,4,16,16,256]{4,3,2,1,0:T(8,128)(2,1)S(1)} %reshap, ...), kind=kLoop, calls=%fused_computation.5 | loop fusion | bytes 11010048 | tf_op jit(solution)/shard_map/slice | solution.py:40
  83.8 0.6 pad_slice_fusion.1
  84.4 1.3 %copy-done.1 = bf16[3,3,3,256,256]{4,3,2,1,0:T(8,128)(2,1)S(1)} copy-done((bf16[3,3,3,256,256]{4,3,2,1,0:T(8,128)(2,1)S(1)}, bf16[3,3,3,256,256]{4,3,2,1,0:T(8,128)(2,1)}, u32[]{:S(2)}) %copy-start.1) | copy-done | bytes 3538968
  85.7 0.6 fusion.1
  86.4 0.6 convolution_add_fusion.7
  87.1 0.6 convolution_add_fusion.6
  87.8 0.6 convolution_add_fusion.5
  88.5 0.6 convolution_add_fusion.4
  89.2 0.6 convolution_add_fusion.3
  89.9 0.6 convolution_add_fusion.2
  90.6 0.6 convolution_add_fusion.1
  91.4 0.6 convolution_add_fusion
  92.0 1.1 %select_convert_fusion = bf16[1,1,2,2,16,16,256]{6,5,4,3,2,1,0:T(8,128)(2,1)} fusion(f32[1,1,2,2,16,16,256]{6,5,4,3,2,1,0:T(8,128)S(1)} %bitcast.193, f32[256]{0:T(256)S(1)} %copy-done.5, pred[2,2,16,16]{3,2,1,0:T(8,128)(4,1)S(1)} %broadcast_and_fusion.2), kind=kLoop, calls=%fused_computation.108 | loop fusion | flops 1835008 | bytes 1574912 | tf_op jit(solution)/shard_map/convert_element_type | solution.py:102
  (93 shorter events, 9.3 us)
Async XLA Ops:
  1.5 19.3 %all-to-all-start = ((bf16[16,2,192]{2,1,0:T(2,128)(2,1)}), bf16[16,2,192]{2,1,0:T(2,128)(2,1)S(1)}, u32[]{:S(2)}, u32[]{:S(2)}) async-start(bf16[16,2,192]{2,1,0:T(2,128)(2,1)} %reshape.402), calls=%async_computation | async-start | bytes 32768 | tf_op jit(solution)/shard_map/all_to_all | solution.py:137
  21.0 4.5 %collective-permute-start = (bf16[3,2,16,64]{3,1,0,2:T(2,128)(2,1)S(1)}, bf16[3,2,16,64]{3,1,0,2:T(2,128)(2,1)S(1)}, u32[]{:S(2)}, u32[]{:S(2)}) collective-permute-start(bf16[3,2,16,64]{3,1,0,2:T(2,128)(2,1)S(1)} %bitcast_bitcast_fusion), channel_id=1, source_target_pairs={{0,1},{1,2},{2,3},{3,4},{4,5},{5,6},{6,7},{7,8},{8,9},{9,10},{10,1... | collective-permute-start | bytes 36872 | tf_op jit(solution)/shard_map/ppermute | solution.py:15
  27.0 0.9 %copy-start.2 = (bf16[3,3,3,16,256]{4,3,2,1,0:T(8,128)(2,1)S(1)}, bf16[3,3,3,16,256]{4,3,2,1,0:T(8,128)(2,1)}, u32[]{:S(2)}) copy-start(bf16[3,3,3,16,256]{4,3,2,1,0:T(8,128)(2,1)} %param.18) | copy-start | bytes 663556
  29.8 0.8 copy-start.3
  30.8 6.3 %collective-permute-start.2 = (bf16[3,2,8,8,256]{4,3,2,1,0:T(8,128)(2,1)S(1)}, bf16[3,2,8,8,256]{4,3,2,1,0:T(8,128)(2,1)S(1)}, u32[]{:S(2)}, u32[]{:S(2)}) collective-permute-start(bf16[3,2,8,8,256]{4,3,2,1,0:T(8,128)(2,1)S(1)} %select_convert_fusion.2), channel_id=1, source_target_pairs={{0,1},{1,2},{2,3},{3,4},{4,5},{5,6},{6,7},{7,8},{8,9},{9,10},{10,1... | collective-permute-start | bytes 589832 | tf_op jit(solution)/shard_map/ppermute | solution.py:15
  31.0 10.7 %collective-permute-start.1 = (bf16[3,2,8,8,256]{4,3,2,1,0:T(8,128)(2,1)S(1)}, bf16[3,2,8,8,256]{4,3,2,1,0:T(8,128)(2,1)S(1)}, u32[]{:S(2)}, u32[]{:S(2)}) collective-permute-start(bf16[3,2,8,8,256]{4,3,2,1,0:T(8,128)(2,1)S(1)} %select_convert_fusion.2), channel_id=1, source_target_pairs={{0,2},{1,3},{2,4},{3,5},{4,6},{5,7},{6,8},{7,9},{8,10},{9,11},{10,... | collective-permute-start | bytes 589832 | tf_op jit(solution)/shard_map/ppermute | solution.py:15
  42.8 27.9 %collective-permute-start.3 = (bf16[2,98304]{1,0:T(2,128)(2,1)S(1)}, bf16[2,98304]{1,0:T(2,128)(2,1)S(1)}, u32[]{:S(2)}, u32[]{:S(2)}) collective-permute-start(bf16[2,98304]{1,0:T(2,128)(2,1)S(1)} %convolution_convert_fusion.1), channel_id=1, source_target_pairs={{0,256},{16,272},{32,288},{48,304},{64,320},{80,336},{96,352},{112... | collective-permute-start | bytes 1179656 | tf_op jit(solution)/shard_map/ppermute | solution.py:15
  72.4 2.0 %copy-start = (bf16[3,3,3,256,256]{4,3,2,1,0:T(8,128)(2,1)S(1)}, bf16[3,3,3,256,256]{4,3,2,1,0:T(8,128)(2,1)}, u32[]{:S(2)}) copy-start(bf16[3,3,3,256,256]{4,3,2,1,0:T(8,128)(2,1)} %param.20) | copy-start | bytes 10616836
  77.9 0.7 copy-start.4
  83.7 2.0 %copy-start.1 = (bf16[3,3,3,256,256]{4,3,2,1,0:T(8,128)(2,1)S(1)}, bf16[3,3,3,256,256]{4,3,2,1,0:T(8,128)(2,1)}, u32[]{:S(2)}) copy-start(bf16[3,3,3,256,256]{4,3,2,1,0:T(8,128)(2,1)} %param.22) | copy-start | bytes 10616836
  91.3 0.7 copy-start.5
where the time goes:
time: 93.7 us; the launch traced here: 93.2 us
  waiting for transfers between devices  28.7 us (31%)
  starting transfers between devices  20.4 us (22%)
  local copies, waits for them, and re-layouts  19.1 us (20%)
  other arithmetic  12.6 us (13%)
  matrix products  11.5 us (12%)
    ppermute x4, waiting for transfers between devices, passed_along(): lax.ppermute(value, axis, [(i, (i + by) % peers) for i in range(peers)])  28.7 us
    ppermute x4, starting transfers between devices, passed_along(): lax.ppermute(value, axis, [(i, (i + by) % peers) for i in range(peers)])  13.2 us
    dot_general x27, matrix products, causal_conv(): jnp.dot(stacked.reshape(-1, 3 * in_chans), kernel[row_tap, col_tap], pref...  10.2 us
    all_to_all x1, starting transfers between devices, body(): lax.all_to_all(local_tokens.reshape(tiles_per, seq_count, TF, patch_part,...  7.21 us
    slice x6, local copies, waits for them, and re-layouts, causal_conv(): window[:, time_tap:time_tap + out_frames]  5.65 us
    unnamed x17, local copies, waits for them, and re-layouts  5.63 us
    mul x1, other arithmetic, region(): scale * row_limit  3.74 us
    concatenate x27, other arithmetic, causal_conv(): jnp.concatenate([window[:, time_tap:time_tap + out_frames] for time_tap i...  2.59 us
  transfers between devices with their start and end apart: 5, of which 4 were waited for; matrix products, arithmetic and copies ran while one was open for 14% of the time, Pallas kernels for 0%

commit v1 on v0

v1 whole, which is shorter than its diff:
```python
import functools

import jax
import jax.numpy as jnp
from jax import lax
from jax.experimental import pallas as pl
from jax.experimental.pallas import tpu as pltpu
from jax.sharding import PartitionSpec as P

F32 = jnp.float32
BF16 = jnp.bfloat16
I32 = jnp.int32
CH = 256
SEQ = 16
TILES = 3
VMEM_LIMIT = 56 * 1024 * 1024


def iota(shape, dim):
    return lax.broadcasted_iota(I32, shape, dim)


def one(mask):
    return jnp.where(mask, 1.0, 0.0).astype(BF16)


def prep_kernel(
    frames_ref,
    heights_ref,
    widths_ref,
    device_ref,
    slot_ref,
    stem_ref,
    second_ref,
    pick_ref,
    place_ref,
    limits_ref,
    lanes_ref,
    spread_ref,
    stem_out_ref,
    folded_ref,
):
    me = lax.axis_index("req")
    column = lax.axis_index("seq")
    half = frames_ref.shape[1] // 2
    partner = lax.rem(me + half, 2 * half)

    lane = iota((1, 32), 1)

    def entry(ref, who):
        return jnp.sum(jnp.where(lane == who, ref[...], 0), axis=1, keepdims=True)

    dest = iota((SEQ, 1), 0)
    tile_lane = iota((SEQ, 32), 1)

    def of_request(ref, tile, who):
        return jnp.sum(jnp.where(tile_lane == who, ref[tile], 0), axis=1, keepdims=True)

    codes = []
    lims = []
    tops = []
    for k in range(2):
        code = jnp.zeros((SEQ, 1), I32)
        live = jnp.zeros((SEQ, 1), I32)
        taken = jnp.zeros((SEQ, 1), I32)
        for i in range(TILES):
            start = 32 * i + 2 * dest - 6
            for who, offset in ((me, 0), (partner, 128)):
                hit = (of_request(device_ref, i, who) == me) & (
                    of_request(slot_ref, i, who) == k
                )
                code = code + jnp.where(hit, start + offset, 0)
                live = live + jnp.where(hit, 1, 0)
                if offset:
                    taken = taken + jnp.where(hit, 1, 0)
        lim = jnp.where(
            taken > 0,
            128 + entry(frames_ref, partner),
            jnp.where(live > 0, entry(frames_ref, me), 0),
        )
        code = jnp.where(live > 0, code, -64)
        codes.append(code)
        lims.append(lim)
        mine = dest == column

        def at_mine(v, mine=mine):
            return jnp.sum(jnp.where(mine, v, 0), axis=0, keepdims=True)

        my_taken = at_mine(taken) > 0
        my_live = at_mine(live) > 0
        tops.append(
            (
                jnp.where(my_taken, entry(heights_ref, partner), entry(heights_ref, me)),
                jnp.where(my_taken, entry(widths_ref, partner), entry(widths_ref, me)),
                at_mine(code) - jnp.where(my_taken, 128, 0),
                jnp.where(
                    my_live,
                    jnp.where(my_taken, entry(frames_ref, partner), entry(frames_ref, me)),
                    -64,
                ),
            )
        )

    source = iota((SEQ, 256), 1)
    for h in range(2):
        for k in range(2):
            for pair in range(4):
                row = (h * 8 + k * 4 + pair) * SEQ
                pick_ref[row : row + SEQ, :] = one(
                    (source == codes[k] + (2 * pair + h)) & (source < lims[k])
                )

    second_slot = iota((16, 128), 0) >= 8
    for n in range(4):
        limits_ref[n] = jnp.where(second_slot, tops[1][n], tops[0][n])

    row = iota((384, 128), 0)
    col = iota((384, 128), 1)
    tap = row >> 7
    y = (row >> 4) & 7
    which = (row >> 3) & 1
    x = (row & 7) + tap - 1
    tall = jnp.where(which == 1, tops[1][0], tops[0][0])
    wide = jnp.where(which == 1, tops[1][1], tops[0][1])
    wanted = ((y & 1) * 2 + (x & 1)) * 32 + which * 16 + (y >> 1) * 4 + (x >> 1)
    place_ref[...] = one((col == wanted) & (y < tall) & (x >= 0) & (x < wide))

    row = iota((512, 512), 0)
    col = iota((512, 512), 1)
    lanes_ref[...] = one(col == (row & 3) * 128 + (row >> 6) * 16 + ((row >> 2) & 15))

    row = iota((256, 768), 0)
    col = iota((256, 768), 1)
    step = (col >> 4) & 3
    spread_ref[...] = one(
        (row >> 7 == (col >> 6) & 1)
        & (step < 3)
        & ((row >> 4) & 7 == (col >> 7) + step)
        & (row & 15 == col & 15)
    )

    stem_out_ref[...] = jnp.zeros(stem_out_ref.shape, BF16)
    for dy in range(3):
        for dx in range(3):
            stem_out_ref[dy, dx * 64 : dx * 64 + 48, :] = stem_ref[dy * 3 + dx]

    def rows_of(u, w, t):
        return second_ref[u, w, t].astype(F32)

    def fold(t, carry):
        by_row = []
        for w in range(3):
            w0, w1, w2 = (rows_of(u, w, t) for u in range(3))
            by_row.append((w0, w1 + w2, w0 + w1, w2))
        for a in range(2):
            for ty in range(2):
                c0, c1, c2 = (by_row[w][2 * a + ty] for w in range(3))
                for b, tx, v in ((0, 0, c0), (0, 1, c1 + c2), (1, 0, c0 + c1), (1, 1, c2)):
                    folded_ref[((a * 2 + b) * 2 + ty) * 2 + tx, t] = v.astype(BF16)
        return carry

    lax.fori_loop(0, 3, fold, 0)


def pick_kernel(own_ref, other_ref, pick_ref, out_ref, rows_ref):
    gap = jnp.zeros((64, 32), BF16)
    both = jnp.concatenate([own_ref[...], gap, other_ref[...], gap], axis=1)
    picked = lax.dot_general(
        pick_ref[...], both, (((1,), (1,)), ((), ())), preferred_element_type=F32
    )
    joined = jnp.concatenate([picked[:128], picked[128:]], axis=1)
    for part in range(8):
        rows_ref[pl.ds(part, SEQ, stride=8), :] = joined[part * SEQ : (part + 1) * SEQ]
    out_ref[...] = rows_ref[...].astype(BF16).reshape(out_ref.shape)


def silu(v):
    halved = 0.5 * v
    return halved + halved * jnp.tanh(halved)


def store_taps(ref, frame, y, value):
    split = value.reshape(2, 8, CH)
    column = iota((2, 8, CH), 1)
    before = jnp.where(column == 0, 0.0, pltpu.roll(split, 1, 1))
    after = jnp.where(column == 7, 0.0, pltpu.roll(split, 7, 1))
    ref[0, frame, y + 1] = before.reshape(16, CH).astype(BF16)
    ref[1, frame, y + 1] = value.astype(BF16)
    ref[2, frame, y + 1] = after.reshape(16, CH).astype(BF16)


def main_kernel(
    tokens_ref,
    place_ref,
    limits_ref,
    lanes_ref,
    spread_ref,
    stem_ref,
    stem_bias_ref,
    first_hbm,
    first_bias_ref,
    folded_ref,
    second_bias_ref,
    out_ref,
    rows_ref,
    taps_ref,
    one_ref,
    two_ref,
    acc_ref,
    first_ref,
    mixed_ref,
    sems,
):
    copies = [
        pltpu.make_async_copy(first_hbm.at[u], first_ref.at[u], sems.at[u]) for u in range(3)
    ]
    for copy in copies:
        copy.start()

    rows_ref[...] = tokens_ref[...].reshape(128, 128).astype(F32)
    window = jnp.concatenate(
        [
            jnp.concatenate(
                [rows_ref[pl.ds(k * 4 + pair, SEQ, stride=8), :] for pair in range(4)], axis=1
            )
            for k in range(2)
        ],
        axis=0,
    ).astype(BF16)
    parity = jnp.dot(window, lanes_ref[...], preferred_element_type=F32).astype(BF16)
    stacked = jnp.concatenate([parity[:, n * 128 : (n + 1) * 128] for n in range(4)], axis=0)
    placed = jnp.dot(place_ref[...], stacked, preferred_element_type=F32).astype(BF16)
    near = jnp.dot(
        jnp.concatenate([placed[:128], placed[128:256]], axis=1),
        spread_ref[...],
        preferred_element_type=F32,
    ).astype(BF16)
    far = jnp.dot(
        placed[256:], spread_ref[:128], preferred_element_type=F32
    ).astype(BF16)
    zero_row = jnp.zeros((16, CH), BF16)
    for g in range(6):
        lanes = slice(g * 128, (g + 1) * 128)
        taps_ref[g, 0] = zero_row
        taps_ref[g, 1:9, :, :128] = near[:, lanes].reshape(8, 16, 128)
        taps_ref[g, 1:9, :, 128:] = far[:, lanes].reshape(8, 16, 128)
        taps_ref[g, 9] = zero_row
        for dx in range(3):
            one_ref[dx, g, 0] = zero_row
            one_ref[dx, g, 9] = zero_row
    for g in range(4):
        for dx in range(3):
            two_ref[dx, g, 0] = zero_row
            two_ref[dx, g, 9] = zero_row

    tall = limits_ref[0]
    wide = limits_ref[1]
    start = limits_ref[2]
    count = limits_ref[3]
    tall = jnp.concatenate([tall, tall], axis=1)
    wide = jnp.concatenate([wide, wide], axis=1)
    start = jnp.concatenate([start, start], axis=1)
    count = jnp.concatenate([count, count], axis=1)
    column = iota((16, CH), 0) & 7
    inside = column < wide

    def finish(frame, offset, y, total, bias, ref):
        value = silu(total + bias)
        keep = inside & (tall > y) & (start + offset + frame >= 0)
        store_taps(ref, frame, y, jnp.where(keep, value, 0.0))

    stem_bias = stem_bias_ref[...]
    hidden = jnp.dot(
        taps_ref[:, 0:8].reshape(768, CH), stem_ref[0], preferred_element_type=F32
    )
    for dy in range(1, 3):
        hidden = hidden + jnp.dot(
            taps_ref[:, dy : dy + 8].reshape(768, CH), stem_ref[dy], preferred_element_type=F32
        )
    hidden = hidden.reshape(6, 8, 16, CH)
    for g in range(6):
        for y in range(8):
            finish(g, 2, y, hidden[g, y], stem_bias, one_ref)

    first_bias = first_bias_ref[...]
    total = None
    for dy in range(3):
        copies[dy].wait()
        for dx in range(3):
            for dt in range(3):
                part = jnp.dot(
                    one_ref[dx, dt : dt + 4, dy : dy + 8].reshape(512, CH),
                    first_ref[dy, dx, dt],
                    preferred_element_type=F32,
                )
                total = part if total is None else total + part
    total = total.reshape(4, 8, 16, CH)
    for g in range(4):
        for y in range(8):
            finish(g, 4, y, total[g, y], first_bias, two_ref)

    second_bias = second_bias_ref[...]
    for a in range(2):
        for b in range(2):
            total = None
            for ty in range(2):
                for tx in range(2):
                    for dt in range(3):
                        part = jnp.dot(
                            two_ref[b + tx, dt : dt + 2, a + ty : a + ty + 8].reshape(256, CH),
                            folded_ref[((a * 2 + b) * 2 + ty) * 2 + tx, dt],
                            preferred_element_type=F32,
                        )
                        total = part if total is None else total + part
            total = total.reshape(2, 8, 16, CH)
            for f in range(2):
                for y in range(8):
                    value = silu(total[f, y] + second_bias)
                    keep = inside & (tall > y) & (start + 6 + f < count)
                    value = jnp.where(keep, value, 0.0)
                    for k in range(2):
                        row = ((k * 2 + f) * 16 + 2 * y + a) * 16 + b
                        for side in range(2):
                            mixed_ref[side, pl.ds(row, 8, stride=2), :] = value[
                                k * 8 : k * 8 + 8, side * 128 : side * 128 + 128
                            ]
    for side in range(2):
        out_ref[:, side * 128 : side * 128 + 128] = mixed_ref[side].astype(BF16)


def vmem_spec():
    return pl.BlockSpec(memory_space=pltpu.VMEM)


def body(
    transformer_tokens,
    frames,
    heights,
    widths,
    tile_decode_device,
    tile_device_slot,
    stem_conv_weight,
    stem_conv_bias,
    upsample_first_weight,
    upsample_first_bias,
    upsample_second_weight,
    upsample_second_bias,
):
    requests = lax.axis_size("req")
    half = requests // 2
    own = jnp.transpose(transformer_tokens[0, :, 0, :])
    other = lax.ppermute(own, "req", [(i, (i + half) % requests) for i in range(requests)])
    shape = jax.ShapeDtypeStruct
    pick, place, limits, lanes, spread, stem, folded = pl.pallas_call(
        prep_kernel,
        out_shape=(
            shape((256, 256), BF16),
            shape((384, 128), BF16),
            shape((4, 16, 128), I32),
            shape((512, 512), BF16),
            shape((256, 768), BF16),
            shape((3, 256, CH), BF16),
            shape((16, 3, CH, CH), BF16),
        ),
        in_specs=[vmem_spec()] * 7,
        out_specs=(vmem_spec(),) * 7,
        compiler_params=pltpu.CompilerParams(vmem_limit_bytes=VMEM_LIMIT),
    )(
        frames[None],
        heights[None],
        widths[None],
        jnp.transpose(tile_decode_device, (2, 1, 0)),
        jnp.transpose(tile_device_slot, (2, 1, 0)),
        stem_conv_weight.reshape(9, 48, CH),
        upsample_second_weight,
    )
    sent = pl.pallas_call(
        pick_kernel,
        out_shape=shape((SEQ, 8, 128), BF16),
        in_specs=[vmem_spec()] * 3,
        out_specs=vmem_spec(),
        scratch_shapes=[pltpu.VMEM((128, 128), F32)],
    )(own, other, pick)
    tokens = lax.all_to_all(sent, "seq", 0, 0, tiled=True)
    decoded = pl.pallas_call(
        main_kernel,
        out_shape=shape((1024, CH), BF16),
        in_specs=[vmem_spec()] * 7
        + [pl.BlockSpec(memory_space=pl.ANY)]
        + [vmem_spec()] * 3,
        out_specs=vmem_spec(),
        scratch_shapes=[
            pltpu.VMEM((128, 128), F32),
            pltpu.VMEM((6, 10, 16, CH), BF16),
            pltpu.VMEM((3, 6, 10, 16, CH), BF16),
            pltpu.VMEM((3, 4, 10, 16, CH), BF16),
            pltpu.VMEM((512, CH), F32),
            pltpu.VMEM((3, 3, 3, CH, CH), BF16),
            pltpu.VMEM((2, 1024, 128), F32),
            pltpu.SemaphoreType.DMA((3,)),
        ],
        compiler_params=pltpu.CompilerParams(vmem_limit_bytes=VMEM_LIMIT),
    )(
        tokens,
        place,
        limits,
        lanes,
        spread,
        stem,
        stem_conv_bias[None],
        upsample_first_weight,
        upsample_first_bias[None],
        folded,
        upsample_second_bias[None],
    )
    return decoded.reshape(1, 1, 2, 2, 16, 16, CH)


def solution(mesh):
    placed = (P("req", None, "seq", None), P(), P(), P(), P(), P(), P(), P(), P(), P(), P(), P())
    return jax.shard_map(
        body,
        mesh=mesh,
        in_specs=placed,
        out_specs=P("req", "seq", None, None, None, None, None),
        check_vma=False,
    )
```

time: 93.7 us -> 49.5 us (0.53)
  the two profiles are of different devices: /device:TPU:68 before, /device:TPU:1 now
where the time goes in v1:
time: 49.5 us; the launch traced here: 49.3 us
  Pallas kernels  21.7 us (44%)
  blocking collectives  15.6 us (32%)
  starting transfers between devices  11.5 us (23%)
  local copies, waits for them, and re-layouts  0.6 us (1%)
    all_to_all x1, blocking collectives, body(): tokens = lax.all_to_all(sent, 'seq', 0, 0, tiled=True)  15.6 us
    pallas_call x1, Pallas kernels, body(): pl.pallas_call(main_kernel, out_shape=shape((1024, CH), BF16), in_specs=[...  12.7 us
    ppermute x1, starting transfers between devices, body(): lax.ppermute(own, 'req', [(i, (i + half) % requests) for i in range(reque...  11.5 us
    pallas_call x1, Pallas kernels, body(): pl.pallas_call(prep_kernel, out_shape=(shape((256, 256), BF16), shape((38...  7.18 us
    pallas_call x1, Pallas kernels, body(): pl.pallas_call(pick_kernel, out_shape=shape((SEQ, 8, 128), BF16), in_spec...  1.8 us
  transfers between devices with their start and end apart: 1, of which 0 were waited for; matrix products, arithmetic and copies ran while one was open for 0% of the time, Pallas kernels for 15%

profile of v1, /device:TPU:1, one launch (start us, length us, event | category | flops | bytes accessed | tf_op | source)
XLA Modules:
  0.0 49.3 jit_solution(11979427012515464237)
XLA Ops:
  0.0 11.5 %collective-permute-start = (bf16[64,96]{1,0:T(8,128)(2,1)}, bf16[64,96]{1,0:T(8,128)(2,1)S(1)}, u32[]{:S(2)}, u32[]{:S(2)}) collective-permute-start(bf16[64,96]{1,0:T(8,128)(2,1)} %bitcast.16), channel_id=1, source_target_pairs={{0,256},{16,272},{32,288},{48,304},{64,320},{80,336},{96,352},{112... | collective-permute-start | bytes 36872 | tf_op jit(solution)/shard_map/ppermute | solution.py:352
  11.5 7.2 %shard_map.118 = (bf16[256,256]{1,0:T(8,128)(2,1)}, bf16[384,128]{1,0:T(8,128)(2,1)}, s32[4,16,128]{2,1,0:T(8,128)}, bf16[512,512]{1,0:T(8,128)(2,1)}, bf16[256,...) custom-call(s32[1,32]{1,0:T(1,128)} %bitcast.21, s32[1,32]{1,0:T(1,128)} %bitcast.22, ...), custom_call_target="tpu_custom_call" | custom-call | tf_op jit(solution)/shard_map/pallas_call | solution.py:354
  18.6 0.0 collective-permute-done.other_ref
  18.6 0.0 copy-start
  18.7 0.6 %copy-done = bf16[64,96]{1,0:T(8,128)(2,1)} copy-done((bf16[64,96]{1,0:T(8,128)(2,1)}, bf16[64,96]{1,0:T(8,128)(2,1)S(1)}, u32[]{:S(2)}) %copy-start) | copy-done | bytes 12312
  19.3 1.8 %shard_map.119 = bf16[16,8,128]{2,1,0:T(8,128)(2,1)} custom-call(bf16[64,96]{1,0:T(8,128)(2,1)} %bitcast.17, bf16[64,96]{1,0:T(8,128)(2,1)} %copy-done, bf16[256,256]{1,0:T(8,128)(2,1)} %get-tuple-element.12.pick_ref), custom_call_target="tpu_custom_call" | custom-call | tf_op jit(solution)/shard_map/pallas_call | solution.py:377
  21.1 15.6 %all_to_all.5.tokens_ref = bf16[16,8,128]{2,1,0:T(8,128)(2,1)} all-to-all(bf16[16,8,128]{2,1,0:T(8,128)(2,1)} %shard_map.119), channel_id=1, replica_groups=mesh['req'=32,'seq'=16] {'seq'}, dimensions={0} | all-to-all | bytes 65536 | tf_op jit(solution)/shard_map/all_to_all | solution.py:384
  36.6 12.7 %shard_map.120 = bf16[1024,256]{1,0:T(8,128)(2,1)} custom-call(bf16[16,8,128]{2,1,0:T(8,128)(2,1)} %all_to_all.5.tokens_ref, bf16[384,128]{1,0:T(8,128)(2,1)} %get-tuple-element.13.place_ref, s32[4,16,128]{2,1,0:T(8,128)} %get-tuple-element.14.limits_ref, bf16[512,512]{1,0:T(8,128)(2,1)} %get-tuple-element.15.lanes_ref, ...), custom_call_target="tpu_custom_call" | custom-call | tf_op jit(solution)/shard_map/pallas_call | solution.py:385
Async XLA Ops:
  0.0 18.6 %collective-permute-start = (bf16[64,96]{1,0:T(8,128)(2,1)}, bf16[64,96]{1,0:T(8,128)(2,1)S(1)}, u32[]{:S(2)}, u32[]{:S(2)}) collective-permute-start(bf16[64,96]{1,0:T(8,128)(2,1)} %bitcast.16), channel_id=1, source_target_pairs={{0,256},{16,272},{32,288},{48,304},{64,320},{80,336},{96,352},{112... | collective-permute-start | bytes 36872 | tf_op jit(solution)/shard_map/ppermute | solution.py:352
  18.6 0.6 %copy-start = (bf16[64,96]{1,0:T(8,128)(2,1)}, bf16[64,96]{1,0:T(8,128)(2,1)S(1)}, u32[]{:S(2)}) copy-start(bf16[64,96]{1,0:T(8,128)(2,1)S(1)} %collective-permute-done.other_ref) | copy-start | bytes 36868

commit v2 on v1

--- a/solution.py
+++ b/solution.py
@@ -13,7 +13,7 @@
 CH = 256
 SEQ = 16
 TILES = 3
-VMEM_LIMIT = 56 * 1024 * 1024
+VMEM_LIMIT = 52 * 1024 * 1024
 
 
 def iota(shape, dim):
@@ -24,21 +24,15 @@
     return jnp.where(mask, 1.0, 0.0).astype(BF16)
 
 
-def prep_kernel(
+def plan_kernel(
     frames_ref,
     heights_ref,
     widths_ref,
     device_ref,
     slot_ref,
-    stem_ref,
-    second_ref,
     pick_ref,
     place_ref,
     limits_ref,
-    lanes_ref,
-    spread_ref,
-    stem_out_ref,
-    folded_ref,
 ):
     me = lax.axis_index("req")
     column = lax.axis_index("seq")
@@ -125,6 +119,31 @@
     wanted = ((y & 1) * 2 + (x & 1)) * 32 + which * 16 + (y >> 1) * 4 + (x >> 1)
     place_ref[...] = one((col == wanted) & (y < tall) & (x >= 0) & (x < wide))
 
+
+def fold_kernel(
+    sent_hbm,
+    stem_ref,
+    second_hbm,
+    lanes_ref,
+    spread_ref,
+    stem_out_ref,
+    folded_hbm,
+    second_ref,
+    folded_ref,
+    in_sems,
+    out_sems,
+):
+    ins = [
+        pltpu.make_async_copy(second_hbm.at[:, :, t], second_ref.at[t], in_sems.at[t])
+        for t in range(3)
+    ]
+    outs = [
+        pltpu.make_async_copy(folded_ref.at[t], folded_hbm.at[t], out_sems.at[t])
+        for t in range(3)
+    ]
+    for copy in ins:
+        copy.start()
+
     row = iota((512, 512), 0)
     col = iota((512, 512), 1)
     lanes_ref[...] = one(col == (row & 3) * 128 + (row >> 6) * 16 + ((row >> 2) & 15))
@@ -144,22 +163,26 @@
         for dx in range(3):
             stem_out_ref[dy, dx * 64 : dx * 64 + 48, :] = stem_ref[dy * 3 + dx]
 
-    def rows_of(u, w, t):
-        return second_ref[u, w, t].astype(F32)
-
-    def fold(t, carry):
-        by_row = []
-        for w in range(3):
-            w0, w1, w2 = (rows_of(u, w, t) for u in range(3))
-            by_row.append((w0, w1 + w2, w0 + w1, w2))
-        for a in range(2):
-            for ty in range(2):
-                c0, c1, c2 = (by_row[w][2 * a + ty] for w in range(3))
-                for b, tx, v in ((0, 0, c0), (0, 1, c1 + c2), (1, 0, c0 + c1), (1, 1, c2)):
-                    folded_ref[((a * 2 + b) * 2 + ty) * 2 + tx, t] = v.astype(BF16)
-        return carry
-
-    lax.fori_loop(0, 3, fold, 0)
+    for t in range(3):
+        ins[t].wait()
+
+        def fold(part, carry, t=t):
+            rows = pl.ds(pl.multiple_of(part * 32, 32), 32)
+            by_row = []
+            for w in range(3):
+                w0, w1, w2 = (second_ref[t, u, w, rows, :].astype(F32) for u in range(3))
+                by_row.append((w0, w1 + w2, w0 + w1, w2))
+            for a in range(2):
+                for ty in range(2):
+                    c0, c1, c2 = (by_row[w][2 * a + ty] for w in range(3))
+                    for b, tx, v in ((0, 0, c0), (0, 1, c1 + c2), (1, 0, c0 + c1), (1, 1, c2)):
+                        folded_ref[t, a * 2 + b, ty * 2 + tx, rows, :] = v.astype(BF16)
+            return carry
+
+        lax.fori_loop(0, CH // 32, fold, 0)
+        outs[t].start()
+    for copy in outs:
+        copy.wait()
 
 
 def pick_kernel(own_ref, other_ref, pick_ref, out_ref, rows_ref):
@@ -199,22 +222,25 @@
     stem_bias_ref,
     first_hbm,
     first_bias_ref,
-    folded_ref,
+    folded_hbm,
     second_bias_ref,
     out_ref,
     rows_ref,
     taps_ref,
     one_ref,
     two_ref,
-    acc_ref,
     first_ref,
+    folded_ref,
     mixed_ref,
     sems,
 ):
     copies = [
         pltpu.make_async_copy(first_hbm.at[u], first_ref.at[u], sems.at[u]) for u in range(3)
     ]
-    for copy in copies:
+    fetches = [
+        pltpu.make_async_copy(folded_hbm.at[t], folded_ref.at[t], sems.at[3 + t]) for t in range(3)
+    ]
+    for copy in copies + fetches:
         copy.start()
 
     rows_ref[...] = tokens_ref[...].reshape(128, 128).astype(F32)
@@ -299,6 +325,8 @@
         for y in range(8):
             finish(g, 4, y, total[g, y], first_bias, two_ref)
 
+    for copy in fetches:
+        copy.wait()
     second_bias = second_bias_ref[...]
     for a in range(2):
         for b in range(2):
@@ -308,7 +336,7 @@
                     for dt in range(3):
                         part = jnp.dot(
                             two_ref[b + tx, dt : dt + 2, a + ty : a + ty + 8].reshape(256, CH),
-                            folded_ref[((a * 2 + b) * 2 + ty) * 2 + tx, dt],
+                            folded_ref[dt, a * 2 + b, ty * 2 + tx],
                             preferred_element_type=F32,
                         )
                         total = part if total is None else total + part
@@ -328,8 +356,71 @@
         out_ref[:, side * 128 : side * 128 + 128] = mixed_ref[side].astype(BF16)
 
 
+def held(value):
+    return pltpu.with_memory_space_constraint(value, pltpu.VMEM)
+
+
 def vmem_spec():
     return pl.BlockSpec(memory_space=pltpu.VMEM)
+
+
+def hbm_spec():
+    return pl.BlockSpec(memory_space=pl.ANY)
+
+
+def fold(sent, stem_weight, second_weight):
+    return pl.pallas_call(
+        fold_kernel,
+        out_shape=(
+            pltpu.VMEM((512, 512), BF16),
+            pltpu.VMEM((256, 768), BF16),
+            pltpu.VMEM((3, 256, CH), BF16),
+            jax.ShapeDtypeStruct((3, 4, 4, CH, CH), BF16),
+        ),
+        in_specs=[hbm_spec(), vmem_spec(), hbm_spec()],
+        out_specs=(vmem_spec(),) * 3 + (hbm_spec(),),
+        scratch_shapes=[
+            pltpu.VMEM((3, 3, 3, CH, CH), BF16),
+            pltpu.VMEM((3, 4, 4, CH, CH), BF16),
+            pltpu.SemaphoreType.DMA((3,)),
+            pltpu.SemaphoreType.DMA((3,)),
+        ],
+        compiler_params=pltpu.CompilerParams(vmem_limit_bytes=VMEM_LIMIT),
+    )(sent, stem_weight.reshape(9, 48, CH), second_weight)
+
+
+def decode(
+    tokens, place, limits, lanes, spread, stem, stem_bias, first, first_bias, folded, second_bias
+):
+    return pl.pallas_call(
+        main_kernel,
+        out_shape=jax.ShapeDtypeStruct((1024, CH), BF16),
+        in_specs=[vmem_spec()] * 7 + [hbm_spec(), vmem_spec(), hbm_spec(), vmem_spec()],
+        out_specs=vmem_spec(),
+        scratch_shapes=[
+            pltpu.VMEM((128, 128), F32),
+            pltpu.VMEM((6, 10, 16, CH), BF16),
+            pltpu.VMEM((3, 6, 10, 16, CH), BF16),
+            pltpu.VMEM((3, 4, 10, 16, CH), BF16),
+            pltpu.VMEM((3, 3, 3, CH, CH), BF16),
+            pltpu.VMEM((3, 4, 4, CH, CH), BF16),
+            pltpu.VMEM((2, 1024, 128), F32),
+            pltpu.SemaphoreType.DMA((6,)),
+        ],
+        compiler_params=pltpu.CompilerParams(vmem_limit_bytes=VMEM_LIMIT),
+    )(
+        tokens,
+        place,
+        limits,
+        lanes,
+        spread,
+        stem,
+        stem_bias[None],
+        first,
+        first_bias[None],
+        folded,
+        second_bias[None],
+    )
 
 
 def body(
@@ -351,28 +442,23 @@
     own = jnp.transpose(transformer_tokens[0, :, 0, :])
     other = lax.ppermute(own, "req", [(i, (i + half) % requests) for i in range(requests)])
     shape = jax.ShapeDtypeStruct
-    pick, place, limits, lanes, spread, stem, folded = pl.pallas_call(
-        prep_kernel,
+    params = pltpu.CompilerParams(vmem_limit_bytes=60 * 1024 * 1024)
+    pick, place, limits = pl.pallas_call(
+        plan_kernel,
         out_shape=(
-            shape((256, 256), BF16),
-            shape((384, 128), BF16),
-            shape((4, 16, 128), I32),
-            shape((512, 512), BF16),
-            shape((256, 768), BF16),
-            shape((3, 256, CH), BF16),
-            shape((16, 3, CH, CH), BF16),
+            pltpu.VMEM((256, 256), BF16),
+            pltpu.VMEM((384, 128), BF16),
+            pltpu.VMEM((4, 16, 128), I32),
         ),
-        in_specs=[vmem_spec()] * 7,
-        out_specs=(vmem_spec(),) * 7,
-        compiler_params=pltpu.CompilerParams(vmem_limit_bytes=VMEM_LIMIT),
+        in_specs=[vmem_spec()] * 5,
+        out_specs=(vmem_spec(),) * 3,
+        compiler_params=params,
     )(
         frames[None],
         heights[None],
         widths[None],
         jnp.transpose(tile_decode_device, (2, 1, 0)),
         jnp.transpose(tile_device_slot, (2, 1, 0)),
-        stem_conv_weight.reshape(9, 48, CH),
-        upsample_second_weight,
     )
     sent = pl.pallas_call(
         pick_kernel,
@@ -380,38 +466,21 @@
         in_specs=[vmem_spec()] * 3,
         out_specs=vmem_spec(),
         scratch_shapes=[pltpu.VMEM((128, 128), F32)],
-    )(own, other, pick)
+    )(own, held(other), held(pick))
     tokens = lax.all_to_all(sent, "seq", 0, 0, tiled=True)
-    decoded = pl.pallas_call(
-        main_kernel,
-        out_shape=shape((1024, CH), BF16),
-        in_specs=[vmem_spec()] * 7
-        + [pl.BlockSpec(memory_space=pl.ANY)]
-        + [vmem_spec()] * 3,
-        out_specs=vmem_spec(),
-        scratch_shapes=[
-            pltpu.VMEM((128, 128), F32),
-            pltpu.VMEM((6, 10, 16, CH), BF16),
-            pltpu.VMEM((3, 6, 10, 16, CH), BF16),
-            pltpu.VMEM((3, 4, 10, 16, CH), BF16),
-            pltpu.VMEM((512, CH), F32),
-            pltpu.VMEM((3, 3, 3, CH, CH), BF16),
-            pltpu.VMEM((2, 1024, 128), F32),
-            pltpu.SemaphoreType.DMA((3,)),
-        ],
-        compiler_params=pltpu.CompilerParams(vmem_limit_bytes=VMEM_LIMIT),
-    )(
-        tokens,
-        place,
-        limits,
-        lanes,
-        spread,
-        stem,
-        stem_conv_bias[None],
+    lanes, spread, stem, folded = fold(sent, stem_conv_weight, upsample_second_weight)
+    decoded = decode(
+        held(tokens),
+        held(place),
+        held(limits),
+        held(lanes),
+        held(spread),
+        held(stem),
+        stem_conv_bias,
         upsample_first_weight,
-        upsample_first_bias[None],
+        upsample_first_bias,
         folded,
-        upsample_second_bias[None],
+        upsample_second_bias,
     )
     return decoded.reshape(1, 1, 2, 2, 16, 16, CH)
 

time: 49.5 us -> 40.6 us (0.82)
  blocking collectives: 15.6 us -> 0 us
  starting transfers between devices: 11.5 us -> 20.2 us
  Pallas kernels: 21.7 us -> 16.8 us
  waiting for transfers between devices: 0.01 us -> 1.35 us
  local copies, waits for them, and re-layouts: 0.6 us -> 1.73 us
    all_to_all x1 -> x0, blocking collectives: 15.6 us -> none  [body(): tokens = lax.all_to_all(sent, 'seq', 0, 0, tiled=True)]
    all_to_all x0 -> x1, starting transfers between devices: none -> 8.64 us  [body(): tokens = lax.all_to_all(sent, 'seq', 0, 0, tiled=True)]
    pallas_call x2 -> x3, Pallas kernels: 19.9 us -> 15.3 us  [the longest x1 9.62 us: decode(): pl.pallas_call(main_kernel, out_shape=jax.ShapeDtypeStruct((1024, CH), BF...]
    all_to_all x0 -> x1, waiting for transfers between devices: none -> 1.35 us  [body(): tokens = lax.all_to_all(sent, 'seq', 0, 0, tiled=True)]
    unnamed x2 -> x10, local copies, waits for them, and re-layouts: 0.6 us -> 1.73 us
  transfers between devices with their start and end apart: 1 -> 2, of which waited for: 0 -> 1; matrix products, arithmetic and copies ran while one was open for 0% -> 0% of each run, Pallas kernels for 15% -> 14%
where the time goes in v2:
time: 40.6 us; the launch traced here: 40.2 us
  starting transfers between devices  20.2 us (50%)
  Pallas kernels  16.8 us (41%)
  local copies, waits for them, and re-layouts  1.73 us (4%)
  waiting for transfers between devices  1.35 us (3%)
    ppermute x1, starting transfers between devices, body(): lax.ppermute(own, 'req', [(i, (i + half) % requests) for i in range(reque...  11.6 us
    pallas_call x1, Pallas kernels, decode(): pl.pallas_call(main_kernel, out_shape=jax.ShapeDtypeStruct((1024, CH), BF...  9.62 us
    all_to_all x1, starting transfers between devices, body(): tokens = lax.all_to_all(sent, 'seq', 0, 0, tiled=True)  8.64 us
    pallas_call x1, Pallas kernels, fold(): pl.pallas_call(fold_kernel, out_shape=(pltpu.VMEM((512, 512), BF16), pltp...  4.31 us
    unnamed x10, local copies, waits for them, and re-layouts  1.73 us
    pallas_call x1, Pallas kernels, body(): pl.pallas_call(pick_kernel, out_shape=shape((SEQ, 8, 128), BF16), in_spec...  1.58 us
    all_to_all x1, waiting for transfers between devices, body(): tokens = lax.all_to_all(sent, 'seq', 0, 0, tiled=True)  1.35 us
    pallas_call x1, Pallas kernels, body(): pl.pallas_call(plan_kernel, out_shape=(pltpu.VMEM((256, 256), BF16), pltp...  1.34 us
  transfers between devices with their start and end apart: 2, of which 1 were waited for; matrix products, arithmetic and copies ran while one was open for 0% of the time, Pallas kernels for 14%

profile of v2, /device:TPU:1, one launch (start us, length us, event | category | flops | bytes accessed | tf_op | source)
XLA Modules:
  0.0 40.2 jit_solution(10648344105814904194)
XLA Ops:
  0.0 0.0 copy-start.4
  0.0 0.0 copy-start.3
  0.0 0.0 copy-start.2
  0.0 11.6 %collective-permute-start = (bf16[64,96]{1,0:T(8,128)(2,1)}, bf16[64,96]{1,0:T(8,128)(2,1)S(1)}, u32[]{:S(2)}, u32[]{:S(2)}) collective-permute-start(bf16[64,96]{1,0:T(8,128)(2,1)} %bitcast.19), channel_id=1, source_target_pairs={{0,256},{16,272},{32,288},{48,304},{64,320},{80,336},{96,352},{112... | collective-permute-start | bytes 36872 | tf_op jit(solution)/shard_map/ppermute | solution.py:443
  11.6 1.3 %shard_map.118 = (bf16[256,256]{1,0:T(8,128)(2,1)S(1)}, bf16[384,128]{1,0:T(8,128)(2,1)S(1)}, s32[4,16,128]{2,1,0:T(8,128)S(1)}) custom-call(s32[1,32]{1,0:T(1,128)} %bitcast.21, s32[1,32]{1,0:T(1,128)} %bitcast.22, s32[1,32]{1,0:T(1,128)} %bitcast.23, s32[3,16,32]{2,1,0:T(8,128)} %bitcast.17, s32[3,16,32]{2,1,0:T(8,128)} %bitcast.18), custom_call_target="tpu_custom_call" | custom-call | tf_op jit(solution)/shard_map/pallas_call | solution.py:446
  13.0 0.0 collective-permute-done.other_ref
  13.0 1.6 %shard_map.119.sent_hbm = bf16[16,8,128]{2,1,0:T(8,128)(2,1)} custom-call(bf16[64,96]{1,0:T(8,128)(2,1)} %bitcast.20, bf16[64,96]{1,0:T(8,128)(2,1)S(1)} %collective-permute-done.other_ref, bf16[256,256]{1,0:T(8,128)(2,1)S(1)} %get-tuple-element.12.pick_ref), custom_call_target="tpu_custom_call" | custom-call | tf_op jit(solution)/shard_map/pallas_call | solution.py:463
  14.6 8.6 %all-to-all-start = ((bf16[16,8,128]{2,1,0:T(8,128)(2,1)}), bf16[16,8,128]{2,1,0:T(8,128)(2,1)S(1)}, u32[]{:S(2)}, u32[]{:S(2)}) async-start(bf16[16,8,128]{2,1,0:T(8,128)(2,1)} %shard_map.119.sent_hbm), calls=%async_computation | async-start | bytes 65536 | tf_op jit(solution)/shard_map/all_to_all | solution.py:470
  23.2 0.0 copy-start
  23.2 0.8 %copy-done = bf16[16,8,128]{2,1,0:T(8,128)(2,1)S(1)} copy-done((bf16[16,8,128]{2,1,0:T(8,128)(2,1)S(1)}, bf16[16,8,128]{2,1,0:T(8,128)(2,1)}, u32[]{:S(2)}) %copy-start) | copy-done | bytes 32792
  24.0 0.0 copy-start.1
  24.0 0.9 %copy-done.1 = bf16[3,3,3,16,256]{4,3,2,1,0:T(8,128)(2,1)S(1)} copy-done((bf16[3,3,3,16,256]{4,3,2,1,0:T(8,128)(2,1)S(1)}, bf16[3,3,3,16,256]{4,3,2,1,0:T(8,128)(2,1)}, u32[]{:S(2)}) %copy-start.1) | copy-done | bytes 221208
  24.9 4.3 %shard_map.120 = (bf16[512,512]{1,0:T(8,128)(2,1)S(1)}, bf16[256,768]{1,0:T(8,128)(2,1)S(1)}, bf16[3,256,256]{2,1,0:T(8,128)(2,1)S(1)}, bf16[3,4,4,256,256]{4,3,2,1,0:T(8,128)(2,1)}) custom-call(bf16[16,8,128]{2,1,0:T(8,128)(2,1)S(1)} %copy-done, bf16[9,48,256]{2,1,0:T(8,128)(2,1)S(1)} %bitcast.13, bf16[3,3,3,256,256]{4,3,2,1,0:T(8,128)(2,1)} %second_hbm.1), custom_call_target="tpu_custom_call" | custom-call | tf_op jit(solution)/shard_map/pallas_call | solution.py:372
  29.2 1.3 %all-to-all-done.tokens_ref = bf16[16,8,128]{2,1,0:T(8,128)(2,1)S(1)} async-done(((bf16[16,8,128]{2,1,0:T(8,128)(2,1)}), bf16[16,8,128]{2,1,0:T(8,128)(2,1)S(1)}, u32[]{:S(2)}, u32[]{:S(2)}) %all-to-all-start) | async-done | bytes 32800 | tf_op jit(solution)/shard_map/all_to_all | solution.py:470
  30.6 0.0 copy-done.4
  30.6 0.0 copy-done.3
  30.6 0.0 copy-done.2
  30.6 9.6 %shard_map.121 = bf16[1024,256]{1,0:T(8,128)(2,1)} custom-call(bf16[16,8,128]{2,1,0:T(8,128)(2,1)S(1)} %all-to-all-done.tokens_ref, bf16[384,128]{1,0:T(8,128)(2,1)S(1)} %get-tuple-element.13.place_ref, s32[4,16,128]{2,1,0:T(8,128)S(1)} %get-tuple-element.14.limits_ref, bf16[512,512]{1,0:T(8,128)(2,1)S(1)} %get-tuple-element.15.lanes_ref, ...), custom_call_target="tpu_custom_call" | custom-call | tf_op jit(solution)/shard_map/pallas_call | solution.py:395
Async XLA Ops:
  0.0 30.6 %copy-start.4 = (f32[256]{0:T(256)S(1)}, f32[256]{0:T(256)}, u32[]{:S(2)}) copy-start(f32[256]{0:T(256)} %param.23) | copy-start | bytes 3076
  0.0 30.6 %copy-start.3 = (f32[256]{0:T(256)S(1)}, f32[256]{0:T(256)}, u32[]{:S(2)}) copy-start(f32[256]{0:T(256)} %param.21) | copy-start | bytes 3076
  0.0 30.6 %copy-start.2 = (f32[256]{0:T(256)S(1)}, f32[256]{0:T(256)}, u32[]{:S(2)}) copy-start(f32[256]{0:T(256)} %param.19) | copy-start | bytes 3076
  0.0 13.0 %collective-permute-start = (bf16[64,96]{1,0:T(8,128)(2,1)}, bf16[64,96]{1,0:T(8,128)(2,1)S(1)}, u32[]{:S(2)}, u32[]{:S(2)}) collective-permute-start(bf16[64,96]{1,0:T(8,128)(2,1)} %bitcast.19), channel_id=1, source_target_pairs={{0,256},{16,272},{32,288},{48,304},{64,320},{80,336},{96,352},{112... | collective-permute-start | bytes 36872 | tf_op jit(solution)/shard_map/ppermute | solution.py:443
  14.6 16.0 %all-to-all-start = ((bf16[16,8,128]{2,1,0:T(8,128)(2,1)}), bf16[16,8,128]{2,1,0:T(8,128)(2,1)S(1)}, u32[]{:S(2)}, u32[]{:S(2)}) async-start(bf16[16,8,128]{2,1,0:T(8,128)(2,1)} %shard_map.119.sent_hbm), calls=%async_computation | async-start | bytes 65536 | tf_op jit(solution)/shard_map/all_to_all | solution.py:470
  23.2 0.8 %copy-start = (bf16[16,8,128]{2,1,0:T(8,128)(2,1)S(1)}, bf16[16,8,128]{2,1,0:T(8,128)(2,1)}, u32[]{:S(2)}) copy-start(bf16[16,8,128]{2,1,0:T(8,128)(2,1)} %shard_map.119.sent_hbm) | copy-start | bytes 98308
  24.0 0.9 %copy-start.1 = (bf16[3,3,3,16,256]{4,3,2,1,0:T(8,128)(2,1)S(1)}, bf16[3,3,3,16,256]{4,3,2,1,0:T(8,128)(2,1)}, u32[]{:S(2)}) copy-start(bf16[3,3,3,16,256]{4,3,2,1,0:T(8,128)(2,1)} %param.18) | copy-start | bytes 663556

commit v3 on v2

--- a/solution.py
+++ b/solution.py
@@ -32,7 +32,6 @@
     slot_ref,
     pick_ref,
     place_ref,
-    limits_ref,
 ):
     me = lax.axis_index("req")
     column = lax.axis_index("seq")
@@ -106,7 +105,9 @@
 
     second_slot = iota((16, 128), 0) >= 8
     for n in range(4):
-        limits_ref[n] = jnp.where(second_slot, tops[1][n], tops[0][n])
+        place_ref[384 + 16 * n : 400 + 16 * n, :] = (
+            jnp.where(second_slot, tops[1][n], tops[0][n]).astype(F32).astype(BF16)
+        )
 
     row = iota((384, 128), 0)
     col = iota((384, 128), 1)
@@ -117,33 +118,10 @@
     tall = jnp.where(which == 1, tops[1][0], tops[0][0])
     wide = jnp.where(which == 1, tops[1][1], tops[0][1])
     wanted = ((y & 1) * 2 + (x & 1)) * 32 + which * 16 + (y >> 1) * 4 + (x >> 1)
-    place_ref[...] = one((col == wanted) & (y < tall) & (x >= 0) & (x < wide))
-
-
-def fold_kernel(
-    sent_hbm,
-    stem_ref,
-    second_hbm,
-    lanes_ref,
-    spread_ref,
-    stem_out_ref,
-    folded_hbm,
-    second_ref,
-    folded_ref,
-    in_sems,
-    out_sems,
-):
-    ins = [
-        pltpu.make_async_copy(second_hbm.at[:, :, t], second_ref.at[t], in_sems.at[t])
-        for t in range(3)
-    ]
-    outs = [
-        pltpu.make_async_copy(folded_ref.at[t], folded_hbm.at[t], out_sems.at[t])
-        for t in range(3)
-    ]
-    for copy in ins:
-        copy.start()
-
+    place_ref[:384, :] = one((col == wanted) & (y < tall) & (x >= 0) & (x < wide))
+
+
+def constants_kernel(sent_hbm, stem_ref, lanes_ref, spread_ref, stem_out_ref):
     row = iota((512, 512), 0)
     col = iota((512, 512), 1)
     lanes_ref[...] = one(col == (row & 3) * 128 + (row >> 6) * 16 + ((row >> 2) & 15))
@@ -163,7 +141,20 @@
         for dx in range(3):
             stem_out_ref[dy, dx * 64 : dx * 64 + 48, :] = stem_ref[dy * 3 + dx]
 
-    for t in range(3):
+
+def fold_kernel(second_hbm, held_ref, folded_hbm, second_ref, folded_ref, in_sems, out_sems):
+    ins = [
+        pltpu.make_async_copy(second_hbm.at[:, :, t], second_ref.at[t], in_sems.at[t])
+        for t in range(3)
+    ]
+    outs = [
+        pltpu.make_async_copy(folded_ref.at[t], folded_hbm.at[t], out_sems.at[t])
+        for t in range(2)
+    ]
+    for t in (1, 2, 0):
+        ins[t].start()
+
+    for t in (1, 2, 0):
         ins[t].wait()
 
         def fold(part, carry, t=t):
@@ -176,16 +167,20 @@
                 for ty in range(2):
                     c0, c1, c2 = (by_row[w][2 * a + ty] for w in range(3))
                     for b, tx, v in ((0, 0, c0), (0, 1, c1 + c2), (1, 0, c0 + c1), (1, 1, c2)):
-                        folded_ref[t, a * 2 + b, ty * 2 + tx, rows, :] = v.astype(BF16)
+                        if t:
+                            folded_ref[t - 1, a * 2 + b, ty * 2 + tx, rows, :] = v.astype(BF16)
+                        else:
+                            held_ref[a * 2 + b, ty * 2 + tx, rows, :] = v.astype(BF16)
             return carry
 
         lax.fori_loop(0, CH // 32, fold, 0)
-        outs[t].start()
+        if t:
+            outs[t - 1].start()
     for copy in outs:
         copy.wait()
 
 
-def pick_kernel(own_ref, other_ref, pick_ref, out_ref, rows_ref):
+def pick_kernel(own_ref, other_ref, pick_ref, folded_hbm, out_ref, rows_ref):
     gap = jnp.zeros((64, 32), BF16)
     both = jnp.concatenate([own_ref[...], gap, other_ref[...], gap], axis=1)
     picked = lax.dot_general(
@@ -212,16 +207,28 @@
     ref[2, frame, y + 1] = after.reshape(16, CH).astype(BF16)
 
 
-def main_kernel(
+def multiply(work):
+    for m, steps in enumerate(work):
+        pltpu.matmul_push_rhs(steps[0][0](), 0, m)
+    for n in range(max(len(steps) for steps in work)):
+        for m, steps in enumerate(work):
+            if n + 1 < len(steps):
+                pltpu.matmul_push_rhs(steps[n + 1][0](), (n + 1) % 2, m)
+            if n < len(steps):
+                for order, (acc, rows) in enumerate(steps[n][1]):
+                    pltpu.matmul_acc_lhs(acc, rows(), load_staged_rhs=n % 2 if order == 0 else None)
+
+
+def main_body(
     tokens_ref,
     place_ref,
-    limits_ref,
     lanes_ref,
     spread_ref,
     stem_ref,
     stem_bias_ref,
     first_hbm,
     first_bias_ref,
+    folded_ready_ref,
     folded_hbm,
     second_bias_ref,
     out_ref,
@@ -233,12 +240,14 @@
     folded_ref,
     mixed_ref,
     sems,
+    *accs,
 ):
+    accs, small = (accs[:4], accs[4:8]), accs[8:]
     copies = [
         pltpu.make_async_copy(first_hbm.at[u], first_ref.at[u], sems.at[u]) for u in range(3)
     ]
     fetches = [
-        pltpu.make_async_copy(folded_hbm.at[t], folded_ref.at[t], sems.at[3 + t]) for t in range(3)
+        pltpu.make_async_copy(folded_hbm.at[t], folded_ref.at[t], sems.at[3 + t]) for t in range(2)
     ]
     for copy in copies + fetches:
         copy.start()
@@ -253,20 +262,71 @@
         ],
         axis=0,
     ).astype(BF16)
-    parity = jnp.dot(window, lanes_ref[...], preferred_element_type=F32).astype(BF16)
-    stacked = jnp.concatenate([parity[:, n * 128 : (n + 1) * 128] for n in range(4)], axis=0)
-    placed = jnp.dot(place_ref[...], stacked, preferred_element_type=F32).astype(BF16)
-    near = jnp.dot(
-        jnp.concatenate([placed[:128], placed[128:256]], axis=1),
-        spread_ref[...],
-        preferred_element_type=F32,
-    ).astype(BF16)
-    far = jnp.dot(
-        placed[256:], spread_ref[:128], preferred_element_type=F32
-    ).astype(BF16)
+    multiply(
+        [
+            [
+                (
+                    lambda m=m, k=k: lanes_ref[k * CH : k * CH + CH, m * CH : m * CH + CH],
+                    [(small[m], lambda k=k: window[:, k * CH : k * CH + CH])],
+                )
+                for k in range(2)
+            ]
+            for m in range(2)
+        ]
+    )
+    parity = [pltpu.matmul_pop(small[m]).astype(BF16) for m in range(2)]
+    blank = jnp.zeros((128, 128), BF16)
+    stacked = jnp.concatenate(
+        [parity[n // 2][:, n % 2 * 128 : n % 2 * 128 + 128] for n in range(4)], axis=0
+    )
+    stacked = jnp.concatenate(
+        [jnp.concatenate([stacked, blank], axis=1), jnp.zeros((128, CH), BF16)], axis=0
+    )
+    multiply(
+        [
+            [
+                (
+                    lambda: stacked,
+                    [
+                        (
+                            accs[m][n],
+                            lambda t=2 * m + n: jnp.concatenate(
+                                [place_ref[t * 128 : t * 128 + 128], blank], axis=1
+                            ),
+                        )
+                        for n in range(2 - m)
+                    ],
+                )
+            ]
+            for m in range(2)
+        ]
+    )
+    placed = [
+        pltpu.matmul_pop(acc)[:, :128].astype(BF16) for acc in (accs[0][0], accs[0][1], accs[1][0])
+    ]
+    joined = (
+        jnp.concatenate(placed[:2], axis=1),
+        jnp.concatenate([placed[2], blank], axis=1),
+    )
+    multiply(
+        [
+            [
+                (
+                    lambda t=t: spread_ref[:, t * CH : t * CH + CH],
+                    [(accs[m][t // 2 * 2 + n], lambda n=n: joined[n]) for n in range(2)],
+                )
+                for t in range(m, 3, 2)
+            ]
+            for m in range(2)
+        ]
+    )
+    spread_out = [
+        [pltpu.matmul_pop(accs[t % 2][t // 2 * 2 + n]).astype(BF16) for n in range(2)] for t in range(3)
+    ]
     zero_row = jnp.zeros((16, CH), BF16)
     for g in range(6):
-        lanes = slice(g * 128, (g + 1) * 128)
+        lanes = slice(g % 2 * 128, g % 2 * 128 + 128)
+        near, far = spread_out[g // 2]
         taps_ref[g, 0] = zero_row
         taps_ref[g, 1:9, :, :128] = near[:, lanes].reshape(8, 16, 128)
         taps_ref[g, 1:9, :, 128:] = far[:, lanes].reshape(8, 16, 128)
@@ -279,10 +339,9 @@
             two_ref[dx, g, 0] = zero_row
             two_ref[dx, g, 9] = zero_row
 
-    tall = limits_ref[0]
-    wide = limits_ref[1]
-    start = limits_ref[2]
-    count = limits_ref[3]
+    tall, wide, start, count = (
+        place_ref[384 + 16 * n : 400 + 16 * n, :].astype(F32).astype(I32) for n in range(4)
+    )
     tall = jnp.concatenate([tall, tall], axis=1)
     wide = jnp.concatenate([wide, wide], axis=1)
     start = jnp.concatenate([start, start], axis=1)
@@ -296,54 +355,91 @@
         store_taps(ref, frame, y, jnp.where(keep, value, 0.0))
 
     stem_bias = stem_bias_ref[...]
-    hidden = jnp.dot(
-        taps_ref[:, 0:8].reshape(768, CH), stem_ref[0], preferred_element_type=F32
-    )
-    for dy in range(1, 3):
-        hidden = hidden + jnp.dot(
-            taps_ref[:, dy : dy + 8].reshape(768, CH), stem_ref[dy], preferred_element_type=F32
-        )
-    hidden = hidden.reshape(6, 8, 16, CH)
-    for g in range(6):
-        for y in range(8):
-            finish(g, 2, y, hidden[g, y], stem_bias, one_ref)
+    multiply(
+        [
+            [
+                (
+                    lambda dy=dy: stem_ref[dy],
+                    [
+                        (accs[m][n], lambda g=3 * m + n, dy=dy: taps_ref[g, dy : dy + 8].reshape(128, CH))
+                        for n in range(3)
+                    ],
+                )
+                for dy in range(3)
+            ]
+            for m in range(2)
+        ]
+    )
+    for n in range(3):
+        for m in range(2):
+            hidden = pltpu.matmul_pop(accs[m][n]).reshape(8, 16, CH)
+            for y in range(8):
+                finish(3 * m + n, 2, y, hidden[y], stem_bias, one_ref)
 
     first_bias = first_bias_ref[...]
-    total = None
     for dy in range(3):
         copies[dy].wait()
-        for dx in range(3):
-            for dt in range(3):
-                part = jnp.dot(
-                    one_ref[dx, dt : dt + 4, dy : dy + 8].reshape(512, CH),
-                    first_ref[dy, dx, dt],
-                    preferred_element_type=F32,
+    taps = [(dy, dx, dt) for dy in range(3) for dx in range(3) for dt in range(3)]
+    multiply(
+        [
+            [
+                (
+                    lambda tap=tap: first_ref[tap],
+                    [
+                        (
+                            accs[m][n],
+                            lambda n=n, tap=tap: one_ref[
+                                tap[1], tap[2] + n, tap[0] : tap[0] + 8
+                            ].reshape(128, CH),
+                        )
+                        for n in range(4)
+                    ],
                 )
-                total = part if total is None else total + part
-    total = total.reshape(4, 8, 16, CH)
+                for tap in taps[m::2]
+            ]
+            for m in range(2)
+        ]
+    )
     for g in range(4):
+        total = pltpu.matmul_pop(accs[0][g]) + pltpu.matmul_pop(accs[1][g])
+        total = total.reshape(8, 16, CH)
         for y in range(8):
-            finish(g, 4, y, total[g, y], first_bias, two_ref)
+            finish(g, 4, y, total[y], first_bias, two_ref)
 
     for copy in fetches:
         copy.wait()
     second_bias = second_bias_ref[...]
-    for a in range(2):
-        for b in range(2):
-            total = None
-            for ty in range(2):
-                for tx in range(2):
-                    for dt in range(3):
-                        part = jnp.dot(
-                            two_ref[b + tx, dt : dt + 2, a + ty : a + ty + 8].reshape(256, CH),
-                            folded_ref[dt, a * 2 + b, ty * 2 + tx],
-                            preferred_element_type=F32,
-                        )
-                        total = part if total is None else total + part
-            total = total.reshape(2, 8, 16, CH)
+    for b in range(2):
+        multiply(
+            [
+                [
+                    (
+                        lambda a=a, b=b, ty=ty, tx=tx, dt=dt: (
+                            folded_ref.at[dt - 1] if dt else folded_ready_ref
+                        )[a * 2 + b, ty * 2 + tx],
+                        [
+                            (
+                                accs[a][2 * b + f],
+                                lambda f=f, a=a, b=b, ty=ty, tx=tx, dt=dt: two_ref[
+                                    b + tx, dt + f, a + ty : a + ty + 8
+                                ].reshape(128, CH),
+                            )
+                            for f in range(2)
+                        ],
+                    )
+                    for ty in range(2)
+                    for tx in range(2)
+                    for dt in range(3)
+                ]
+                for a in range(2)
+            ]
+        )
+    for b in range(2):
+        for a in range(2):
             for f in range(2):
+                total = pltpu.matmul_pop(accs[a][2 * b + f]).reshape(8, 16, CH)
                 for y in range(8):
-                    value = silu(total[f, y] + second_bias)
+                    value = silu(total[y] + second_bias)
                     keep = inside & (tall > y) & (start + 6 + f < count)
                     value = jnp.where(keep, value, 0.0)
                     for k in range(2):
@@ -356,6 +452,14 @@
         out_ref[:, side * 128 : side * 128 + 128] = mixed_ref[side].astype(BF16)
 
 
+def main_kernel(*refs):
+    pl.run_scoped(
+        functools.partial(main_body, *refs),
+        *[pltpu.ACC(m)((128, CH), F32) for m in range(2) for _ in range(4)],
+        *[pltpu.ACC(m)((32, CH), F32) for m in range(2)],
+    )
+
+
 def held(value):
     return pltpu.with_memory_space_constraint(value, pltpu.VMEM)
 
@@ -368,34 +472,57 @@
     return pl.BlockSpec(memory_space=pl.ANY)
 
 
-def fold(sent, stem_weight, second_weight):
+def fold(second_weight):
     return pl.pallas_call(
         fold_kernel,
+        out_shape=(
+            pltpu.VMEM((4, 4, CH, CH), BF16),
+            jax.ShapeDtypeStruct((2, 4, 4, CH, CH), BF16),
+        ),
+        in_specs=[hbm_spec()],
+        out_specs=(vmem_spec(), hbm_spec()),
+        scratch_shapes=[
+            pltpu.VMEM((3, 3, 3, CH, CH), BF16),
+            pltpu.VMEM((2, 4, 4, CH, CH), BF16),
+            pltpu.SemaphoreType.DMA((3,)),
+            pltpu.SemaphoreType.DMA((2,)),
+        ],
+        compiler_params=pltpu.CompilerParams(vmem_limit_bytes=VMEM_LIMIT),
+    )(second_weight)
+
+
+def constants(sent, stem_weight):
+    return pl.pallas_call(
+        constants_kernel,
         out_shape=(
             pltpu.VMEM((512, 512), BF16),
             pltpu.VMEM((256, 768), BF16),
             pltpu.VMEM((3, 256, CH), BF16),
-            jax.ShapeDtypeStruct((3, 4, 4, CH, CH), BF16),
         ),
-        in_specs=[hbm_spec(), vmem_spec(), hbm_spec()],
-        out_specs=(vmem_spec(),) * 3 + (hbm_spec(),),
-        scratch_shapes=[
-            pltpu.VMEM((3, 3, 3, CH, CH), BF16),
-            pltpu.VMEM((3, 4, 4, CH, CH), BF16),
-            pltpu.SemaphoreType.DMA((3,)),
-            pltpu.SemaphoreType.DMA((3,)),
-        ],
+        in_specs=[hbm_spec(), vmem_spec()],
+        out_specs=(vmem_spec(),) * 3,
         compiler_params=pltpu.CompilerParams(vmem_limit_bytes=VMEM_LIMIT),
-    )(sent, stem_weight.reshape(9, 48, CH), second_weight)
+    )(sent, stem_weight.reshape(9, 48, CH))
 
 
 def decode(
-    tokens, place, limits, lanes, spread, stem, stem_bias, first, first_bias, folded, second_bias
+    tokens,
+    place,
+    lanes,
+    spread,
+    stem,
+    stem_bias,
+    first,
+    first_bias,
+    ready,
+    folded,
+    second_bias,
 ):
     return pl.pallas_call(
         main_kernel,
         out_shape=jax.ShapeDtypeStruct((1024, CH), BF16),
-        in_specs=[vmem_spec()] * 7 + [hbm_spec(), vmem_spec(), hbm_spec(), vmem_spec()],
+        in_specs=[vmem_spec()] * 6
+        + [hbm_spec(), vmem_spec(), vmem_spec(), hbm_spec(), vmem_spec()],
         out_specs=vmem_spec(),
         scratch_shapes=[
             pltpu.VMEM((128, 128), F32),
@@ -403,21 +530,21 @@
             pltpu.VMEM((3, 6, 10, 16, CH), BF16),
             pltpu.VMEM((3, 4, 10, 16, CH), BF16),
             pltpu.VMEM((3, 3, 3, CH, CH), BF16),
-            pltpu.VMEM((3, 4, 4, CH, CH), BF16),
+            pltpu.VMEM((2, 4, 4, CH, CH), BF16),
             pltpu.VMEM((2, 1024, 128), F32),
-            pltpu.SemaphoreType.DMA((6,)),
+            pltpu.SemaphoreType.DMA((5,)),
         ],
         compiler_params=pltpu.CompilerParams(vmem_limit_bytes=VMEM_LIMIT),
     )(
         tokens,
         place,
-        limits,
         lanes,
         spread,
         stem,
         stem_bias[None],
         first,
         first_bias[None],
+        ready,
         folded,
         second_bias[None],
     )
@@ -443,15 +570,14 @@
     other = lax.ppermute(own, "req", [(i, (i + half) % requests) for i in range(requests)])
     shape = jax.ShapeDtypeStruct
     params = pltpu.CompilerParams(vmem_limit_bytes=60 * 1024 * 1024)
-    pick, place, limits = pl.pallas_call(
+    pick, place = pl.pallas_call(
         plan_kernel,
         out_shape=(
             pltpu.VMEM((256, 256), BF16),
-            pltpu.VMEM((384, 128), BF16),
-            pltpu.VMEM((4, 16, 128), I32),
+            pltpu.VMEM((448, 128), BF16),
         ),
         in_specs=[vmem_spec()] * 5,
-        out_specs=(vmem_spec(),) * 3,
+        out_specs=(vmem_spec(),) * 2,
         compiler_params=params,
     )(
         frames[None],
@@ -460,25 +586,27 @@
         jnp.transpose(tile_decode_device, (2, 1, 0)),
         jnp.transpose(tile_device_slot, (2, 1, 0)),
     )
+    ready, folded = fold(upsample_second_weight)
     sent = pl.pallas_call(
         pick_kernel,
-        out_shape=shape((SEQ, 8, 128), BF16),
-        in_specs=[vmem_spec()] * 3,
+        out_shape=pltpu.VMEM((SEQ, 8, 128), BF16),
+        in_specs=[vmem_spec()] * 3 + [hbm_spec()],
         out_specs=vmem_spec(),
         scratch_shapes=[pltpu.VMEM((128, 128), F32)],
-    )(own, held(other), held(pick))
+        compiler_params=pltpu.CompilerParams(vmem_limit_bytes=VMEM_LIMIT),
+    )(held(own), held(other), held(pick), folded)
     tokens = lax.all_to_all(sent, "seq", 0, 0, tiled=True)
-    lanes, spread, stem, folded = fold(sent, stem_conv_weight, upsample_second_weight)
+    lanes, spread, stem = constants(sent, stem_conv_weight)
     decoded = decode(
         held(tokens),
         held(place),
-        held(limits),
         held(lanes),
         held(spread),
         held(stem),
         stem_conv_bias,
         upsample_first_weight,
         upsample_first_bias,
+        held(ready),
         folded,
         upsample_second_bias,
     )

time: 40.6 us -> 41.8 us (1.030)
  waiting for transfers between devices: 1.35 us -> 6.1 us
  Pallas kernels: 16.8 us -> 14.8 us
  local copies, waits for them, and re-layouts: 1.73 us -> 0.93 us
  starting transfers between devices: 20.2 us -> 19.7 us
    all_to_all x1, waiting for transfers between devices: 1.35 us -> 6.09 us  [body(): tokens = lax.all_to_all(sent, 'seq', 0, 0, tiled=True)]
    pallas_call x2 -> x3, Pallas kernels: 5.89 us -> 4.79 us  [the longest x1 3.57 us: fold(): pl.pallas_call(fold_kernel, out_shape=(pltpu.VMEM((4, 4, CH, CH), BF16),...]
    pallas_call x1, Pallas kernels: 9.62 us -> 8.62 us  [decode(): pl.pallas_call(main_kernel, out_shape=jax.ShapeDtypeStruct((1024, CH), BF...]
    unnamed x10 -> x4, local copies, waits for them, and re-layouts: 1.73 us -> 0.93 us
    all_to_all x1, starting transfers between devices: 8.64 us -> 8.07 us  [body(): tokens = lax.all_to_all(sent, 'seq', 0, 0, tiled=True)]
  transfers between devices with their start and end apart: 2 -> 2, of which waited for: 1 -> 1; matrix products, arithmetic and copies ran while one was open for 0% -> 0% of each run, Pallas kernels for 14% -> 13%
where the time goes in v3:
time: 41.8 us; the launch traced here: 41.5 us
  starting transfers between devices  19.7 us (47%)
  Pallas kernels  14.8 us (35%)
  waiting for transfers between devices  6.1 us (15%)
  local copies, waits for them, and re-layouts  0.93 us (2%)
    ppermute x1, starting transfers between devices, body(): lax.ppermute(own, 'req', [(i, (i + half) % requests) for i in range(reque...  11.6 us
    pallas_call x1, Pallas kernels, decode(): pl.pallas_call(main_kernel, out_shape=jax.ShapeDtypeStruct((1024, CH), BF...  8.62 us
    all_to_all x1, starting transfers between devices, body(): tokens = lax.all_to_all(sent, 'seq', 0, 0, tiled=True)  8.07 us
    all_to_all x1, waiting for transfers between devices, body(): tokens = lax.all_to_all(sent, 'seq', 0, 0, tiled=True)  6.09 us
    pallas_call x1, Pallas kernels, fold(): pl.pallas_call(fold_kernel, out_shape=(pltpu.VMEM((4, 4, CH, CH), BF16),...  3.57 us
    pallas_call x1, Pallas kernels, body(): pl.pallas_call(plan_kernel, out_shape=(pltpu.VMEM((256, 256), BF16), pltp...  1.35 us
    unnamed x4, local copies, waits for them, and re-layouts  0.93 us
    pallas_call x1, Pallas kernels, body(): pl.pallas_call(pick_kernel, out_shape=pltpu.VMEM((SEQ, 8, 128), BF16), in...  0.87 us
  transfers between devices with their start and end apart: 2, of which 1 were waited for; matrix products, arithmetic and copies ran while one was open for 0% of the time, Pallas kernels for 13%

profile of v3, /device:TPU:1, one launch (start us, length us, event | category | flops | bytes accessed | tf_op | source)
XLA Modules:
  0.0 41.5 jit_solution(9225213156560745450)
XLA Ops:
  0.0 0.0 copy-start.1
  0.0 11.6 %collective-permute-start = (bf16[64,96]{1,0:T(8,128)(2,1)}, bf16[64,96]{1,0:T(8,128)(2,1)S(1)}, u32[]{:S(2)}, u32[]{:S(2)}) collective-permute-start(bf16[64,96]{1,0:T(8,128)(2,1)} %bitcast.14), channel_id=1, source_target_pairs={{0,256},{16,272},{32,288},{48,304},{64,320},{80,336},{96,352},{112... | collective-permute-start | bytes 36872 | tf_op jit(solution)/shard_map/ppermute | solution.py:570
  11.6 3.6 %shard_map.119 = (bf16[4,4,256,256]{3,2,1,0:T(8,128)(2,1)S(1)}, bf16[2,4,4,256,256]{4,3,2,1,0:T(8,128)(2,1)}) custom-call(bf16[3,3,3,256,256]{4,3,2,1,0:T(8,128)(2,1)} %second_hbm.1), custom_call_target="tpu_custom_call" | custom-call | tf_op jit(solution)/shard_map/pallas_call | solution.py:476
  15.2 1.4 %shard_map.118 = (bf16[256,256]{1,0:T(8,128)(2,1)S(1)}, bf16[448,128]{1,0:T(8,128)(2,1)S(1)}) custom-call(s32[1,32]{1,0:T(1,128)} %bitcast.21, s32[1,32]{1,0:T(1,128)} %bitcast.22, s32[1,32]{1,0:T(1,128)} %bitcast.23, s32[3,16,32]{2,1,0:T(8,128)} %bitcast.16, s32[3,16,32]{2,1,0:T(8,128)} %bitcast.17), custom_call_target="tpu_custom_call" | custom-call | tf_op jit(solution)/shard_map/pallas_call | solution.py:573
  16.5 0.0 collective-permute-done.other_ref
  16.5 0.0 copy-done.1
  16.6 0.9 %shard_map.120.sent_hbm = bf16[16,8,128]{2,1,0:T(8,128)(2,1)} custom-call(bf16[64,96]{1,0:T(8,128)(2,1)S(1)} %bitcast.15, bf16[64,96]{1,0:T(8,128)(2,1)S(1)} %collective-permute-done.other_ref, bf16[256,256]{1,0:T(8,128)(2,1)S(1)} %get-tuple-element.12.pick_ref, bf16[2,4,4,256,256]{4,3,2,1,0:T(8,128)(2,1)} %get-tuple-element.13.folded_hbm.refs_9_), custom_call_target="tpu_custom_call" | custom-call | tf_op jit(solution)/shard_map/pallas_call | solution.py:590
  17.4 8.1 %all-to-all-start = ((bf16[16,8,128]{2,1,0:T(8,128)(2,1)}), bf16[16,8,128]{2,1,0:T(8,128)(2,1)S(1)}, u32[]{:S(2)}, u32[]{:S(2)}) async-start(bf16[16,8,128]{2,1,0:T(8,128)(2,1)} %shard_map.120.sent_hbm), calls=%async_computation | async-start | bytes 65536 | tf_op jit(solution)/shard_map/all_to_all | solution.py:598
  25.5 0.0 copy-start
  25.5 0.9 %copy-done = bf16[3,3,3,16,256]{4,3,2,1,0:T(8,128)(2,1)S(1)} copy-done((bf16[3,3,3,16,256]{4,3,2,1,0:T(8,128)(2,1)S(1)}, bf16[3,3,3,16,256]{4,3,2,1,0:T(8,128)(2,1)}, u32[]{:S(2)}) %copy-start) | copy-done | bytes 221208
  26.4 0.4 shard_map.121
  26.8 6.1 %all-to-all-done.refs_0_ = bf16[16,8,128]{2,1,0:T(8,128)(2,1)S(1)} async-done(((bf16[16,8,128]{2,1,0:T(8,128)(2,1)}), bf16[16,8,128]{2,1,0:T(8,128)(2,1)S(1)}, u32[]{:S(2)}, u32[]{:S(2)}) %all-to-all-start) | async-done | bytes 32800 | tf_op jit(solution)/shard_map/all_to_all | solution.py:598
  32.9 8.6 %shard_map.122 = bf16[1024,256]{1,0:T(8,128)(2,1)} custom-call(bf16[16,8,128]{2,1,0:T(8,128)(2,1)S(1)} %all-to-all-done.refs_0_, bf16[448,128]{1,0:T(8,128)(2,1)S(1)} %get-tuple-element.14.refs_1_, bf16[512,512]{1,0:T(8,128)(2,1)S(1)} %get-tuple-element.15.refs_2_, bf16[256,768]{1,0:T(8,128)(2,1)S(1)} %get-tuple-element.16.refs_3_, ...), custom_call_target="tpu_custom_call" | custom-call | tf_op jit(solution)/shard_map/pallas_call | solution.py:521
Async XLA Ops:
  0.0 16.5 %copy-start.1 = (bf16[1,96,1,64]{1,3,2,0:T(8,128)(2,1)S(1)}, bf16[1,96,1,64]{1,3,2,0:T(8,128)(2,1)}, u32[]{:S(2)}) copy-start(bf16[1,96,1,64]{1,3,2,0:T(8,128)(2,1)} %param.12) | copy-start | bytes 36868
  0.0 16.5 %collective-permute-start = (bf16[64,96]{1,0:T(8,128)(2,1)}, bf16[64,96]{1,0:T(8,128)(2,1)S(1)}, u32[]{:S(2)}, u32[]{:S(2)}) collective-permute-start(bf16[64,96]{1,0:T(8,128)(2,1)} %bitcast.14), channel_id=1, source_target_pairs={{0,256},{16,272},{32,288},{48,304},{64,320},{80,336},{96,352},{112... | collective-permute-start | bytes 36872 | tf_op jit(solution)/shard_map/ppermute | solution.py:570
  17.4 15.5 %all-to-all-start = ((bf16[16,8,128]{2,1,0:T(8,128)(2,1)}), bf16[16,8,128]{2,1,0:T(8,128)(2,1)S(1)}, u32[]{:S(2)}, u32[]{:S(2)}) async-start(bf16[16,8,128]{2,1,0:T(8,128)(2,1)} %shard_map.120.sent_hbm), calls=%async_computation | async-start | bytes 65536 | tf_op jit(solution)/shard_map/all_to_all | solution.py:598
  25.5 0.9 %copy-start = (bf16[3,3,3,16,256]{4,3,2,1,0:T(8,128)(2,1)S(1)}, bf16[3,3,3,16,256]{4,3,2,1,0:T(8,128)(2,1)}, u32[]{:S(2)}) copy-start(bf16[3,3,3,16,256]{4,3,2,1,0:T(8,128)(2,1)} %param.18) | copy-start | bytes 663556

commit v4 on v3

--- a/solution.py
+++ b/solution.py
@@ -13,6 +13,7 @@
 CH = 256
 SEQ = 16
 TILES = 3
+EARLY = 15
 VMEM_LIMIT = 52 * 1024 * 1024
 
 
@@ -121,7 +122,11 @@
     place_ref[:384, :] = one((col == wanted) & (y < tall) & (x >= 0) & (x < wide))
 
 
-def constants_kernel(sent_hbm, stem_ref, lanes_ref, spread_ref, stem_out_ref):
+def constants_kernel(
+    sent_hbm, stem_ref, first_hbm, lanes_ref, spread_ref, stem_out_ref, ready_ref, sem
+):
+    early = pltpu.make_async_copy(first_hbm.at[:EARLY], ready_ref, sem)
+    early.start()
     row = iota((512, 512), 0)
     col = iota((512, 512), 1)
     lanes_ref[...] = one(col == (row & 3) * 128 + (row >> 6) * 16 + ((row >> 2) & 15))
@@ -140,47 +145,10 @@
     for dy in range(3):
         for dx in range(3):
             stem_out_ref[dy, dx * 64 : dx * 64 + 48, :] = stem_ref[dy * 3 + dx]
-
-
-def fold_kernel(second_hbm, held_ref, folded_hbm, second_ref, folded_ref, in_sems, out_sems):
-    ins = [
-        pltpu.make_async_copy(second_hbm.at[:, :, t], second_ref.at[t], in_sems.at[t])
-        for t in range(3)
-    ]
-    outs = [
-        pltpu.make_async_copy(folded_ref.at[t], folded_hbm.at[t], out_sems.at[t])
-        for t in range(2)
-    ]
-    for t in (1, 2, 0):
-        ins[t].start()
-
-    for t in (1, 2, 0):
-        ins[t].wait()
-
-        def fold(part, carry, t=t):
-            rows = pl.ds(pl.multiple_of(part * 32, 32), 32)
-            by_row = []
-            for w in range(3):
-                w0, w1, w2 = (second_ref[t, u, w, rows, :].astype(F32) for u in range(3))
-                by_row.append((w0, w1 + w2, w0 + w1, w2))
-            for a in range(2):
-                for ty in range(2):
-                    c0, c1, c2 = (by_row[w][2 * a + ty] for w in range(3))
-                    for b, tx, v in ((0, 0, c0), (0, 1, c1 + c2), (1, 0, c0 + c1), (1, 1, c2)):
-                        if t:
-                            folded_ref[t - 1, a * 2 + b, ty * 2 + tx, rows, :] = v.astype(BF16)
-                        else:
-                            held_ref[a * 2 + b, ty * 2 + tx, rows, :] = v.astype(BF16)
-            return carry
-
-        lax.fori_loop(0, CH // 32, fold, 0)
-        if t:
-            outs[t - 1].start()
-    for copy in outs:
-        copy.wait()
-
-
-def pick_kernel(own_ref, other_ref, pick_ref, folded_hbm, out_ref, rows_ref):
+    early.wait()
+
+
+def pick_kernel(own_ref, other_ref, pick_ref, out_ref, rows_ref):
     gap = jnp.zeros((64, 32), BF16)
     both = jnp.concatenate([own_ref[...], gap, other_ref[...], gap], axis=1)
     picked = lax.dot_general(
@@ -207,7 +175,7 @@
     ref[2, frame, y + 1] = after.reshape(16, CH).astype(BF16)
 
 
-def multiply(work):
+def multiply(work, beside=()):
     for m, steps in enumerate(work):
         pltpu.matmul_push_rhs(steps[0][0](), 0, m)
     for n in range(max(len(steps) for steps in work)):
@@ -217,6 +185,9 @@
             if n < len(steps):
                 for order, (acc, rows) in enumerate(steps[n][1]):
                     pltpu.matmul_acc_lhs(acc, rows(), load_staged_rhs=n % 2 if order == 0 else None)
+        for step, thunk in beside:
+            if step == n:
+                thunk()
 
 
 def main_body(
@@ -226,10 +197,10 @@
     spread_ref,
     stem_ref,
     stem_bias_ref,
+    ready_ref,
     first_hbm,
     first_bias_ref,
-    folded_ready_ref,
-    folded_hbm,
+    second_hbm,
     second_bias_ref,
     out_ref,
     rows_ref,
@@ -237,17 +208,16 @@
     one_ref,
     two_ref,
     first_ref,
+    second_ref,
     folded_ref,
     mixed_ref,
     sems,
     *accs,
 ):
     accs, small = (accs[:4], accs[4:8]), accs[8:]
-    copies = [
-        pltpu.make_async_copy(first_hbm.at[u], first_ref.at[u], sems.at[u]) for u in range(3)
-    ]
+    copies = [pltpu.make_async_copy(first_hbm.at[EARLY:], first_ref, sems.at[3])]
     fetches = [
-        pltpu.make_async_copy(folded_hbm.at[t], folded_ref.at[t], sems.at[3 + t]) for t in range(2)
+        pltpu.make_async_copy(second_hbm.at[:, :, t], second_ref.at[t], sems.at[t]) for t in range(3)
     ]
     for copy in copies + fetches:
         copy.start()
@@ -342,17 +312,14 @@
     tall, wide, start, count = (
         place_ref[384 + 16 * n : 400 + 16 * n, :].astype(F32).astype(I32) for n in range(4)
     )
-    tall = jnp.concatenate([tall, tall], axis=1)
-    wide = jnp.concatenate([wide, wide], axis=1)
-    start = jnp.concatenate([start, start], axis=1)
-    count = jnp.concatenate([count, count], axis=1)
-    column = iota((16, CH), 0) & 7
-    inside = column < wide
-
-    def finish(frame, offset, y, total, bias, ref):
-        value = silu(total + bias)
-        keep = inside & (tall > y) & (start + offset + frame >= 0)
-        store_taps(ref, frame, y, jnp.where(keep, value, 0.0))
+    tall = jnp.where((iota((16, 128), 0) & 7) < wide, tall, 0)
+
+    def limit(keep):
+        rows = jnp.where(keep, tall, 0)
+        return jnp.concatenate([rows, rows], axis=1)
+
+    def finish(frame, rows, y, total, bias, ref):
+        store_taps(ref, frame, y, jnp.where(rows > y, silu(total + bias), 0.0))
 
     stem_bias = stem_bias_ref[...]
     multiply(
@@ -373,18 +340,47 @@
     for n in range(3):
         for m in range(2):
             hidden = pltpu.matmul_pop(accs[m][n]).reshape(8, 16, CH)
+            rows = limit(start + (2 + 3 * m + n) >= 0)
             for y in range(8):
-                finish(3 * m + n, 2, y, hidden[y], stem_bias, one_ref)
+                finish(3 * m + n, rows, y, hidden[y], stem_bias, one_ref)
 
     first_bias = first_bias_ref[...]
-    for dy in range(3):
-        copies[dy].wait()
     taps = [(dy, dx, dt) for dy in range(3) for dx in range(3) for dt in range(3)]
+    corners = {(0, 0, 0, 0): (0, 0), (0, 1, 0, 1): (0, 2), (1, 0, 1, 0): (2, 0), (1, 1, 1, 1): (2, 2)}
+    sums = [
+        key
+        for key in ((a, b, ty, tx) for a in range(2) for b in range(2) for ty in range(2) for tx in range(2))
+        if key not in corners
+    ]
+
+    def fold(t):
+        fetches[t].wait()
+        for part in range(0, CH, 64):
+            rows = slice(part, part + 64)
+            w = [[second_ref[t, u, v, rows, :] for v in range(3)] for u in range(3)]
+            by_row = [
+                (w[0][v], w[1][v] + w[2][v], w[0][v] + w[1][v], w[2][v]) for v in range(3)
+            ]
+            for place, (a, b, ty, tx) in enumerate(sums):
+                c = [by_row[v][2 * a + ty] for v in range(3)]
+                folded_ref[t, place, rows, :] = (c[0], c[1] + c[2], c[0] + c[1], c[2])[2 * b + tx]
+
+    def weights_of(t, *key):
+        if key in corners:
+            return second_ref[(t,) + corners[key]]
+        return folded_ref[t, sums.index(key)]
+
+    def first_weights(tap):
+        place = tap[0] * 9 + tap[1] * 3 + tap[2]
+        if place == EARLY:
+            copies[0].wait()
+        return ready_ref[place] if place < EARLY else first_ref[place - EARLY]
+
     multiply(
         [
             [
                 (
-                    lambda tap=tap: first_ref[tap],
+                    lambda tap=tap: first_weights(tap),
                     [
                         (
                             accs[m][n],
@@ -398,25 +394,25 @@
                 for tap in taps[m::2]
             ]
             for m in range(2)
-        ]
-    )
+        ],
+    )
+    for t in range(3):
+        fold(t)
     for g in range(4):
         total = pltpu.matmul_pop(accs[0][g]) + pltpu.matmul_pop(accs[1][g])
         total = total.reshape(8, 16, CH)
+        rows = limit(start + (4 + g) >= 0)
         for y in range(8):
-            finish(g, 4, y, total[y], first_bias, two_ref)
-
-    for copy in fetches:
-        copy.wait()
+            finish(g, rows, y, total[y], first_bias, two_ref)
+
     second_bias = second_bias_ref[...]
+    own_rows = [limit(start + (6 + f) < count) for f in range(2)]
     for b in range(2):
         multiply(
             [
                 [
                     (
-                        lambda a=a, b=b, ty=ty, tx=tx, dt=dt: (
-                            folded_ref.at[dt - 1] if dt else folded_ready_ref
-                        )[a * 2 + b, ty * 2 + tx],
+                        lambda a=a, b=b, ty=ty, tx=tx, dt=dt: weights_of(dt, a, b, ty, tx),
                         [
                             (
                                 accs[a][2 * b + f],
@@ -440,8 +436,7 @@
                 total = pltpu.matmul_pop(accs[a][2 * b + f]).reshape(8, 16, CH)
                 for y in range(8):
                     value = silu(total[y] + second_bias)
-                    keep = inside & (tall > y) & (start + 6 + f < count)
-                    value = jnp.where(keep, value, 0.0)
+                    value = jnp.where(own_rows[f] > y, value, 0.0)
                     for k in range(2):
                         row = ((k * 2 + f) * 16 + 2 * y + a) * 16 + b
                         for side in range(2):
@@ -472,37 +467,20 @@
     return pl.BlockSpec(memory_space=pl.ANY)
 
 
-def fold(second_weight):
-    return pl.pallas_call(
-        fold_kernel,
-        out_shape=(
-            pltpu.VMEM((4, 4, CH, CH), BF16),
-            jax.ShapeDtypeStruct((2, 4, 4, CH, CH), BF16),
-        ),
-        in_specs=[hbm_spec()],
-        out_specs=(vmem_spec(), hbm_spec()),
-        scratch_shapes=[
-            pltpu.VMEM((3, 3, 3, CH, CH), BF16),
-            pltpu.VMEM((2, 4, 4, CH, CH), BF16),
-            pltpu.SemaphoreType.DMA((3,)),
-            pltpu.SemaphoreType.DMA((2,)),
-        ],
-        compiler_params=pltpu.CompilerParams(vmem_limit_bytes=VMEM_LIMIT),
-    )(second_weight)
-
-
-def constants(sent, stem_weight):
+def constants(sent, stem_weight, first):
     return pl.pallas_call(
         constants_kernel,
         out_shape=(
             pltpu.VMEM((512, 512), BF16),
             pltpu.VMEM((256, 768), BF16),
             pltpu.VMEM((3, 256, CH), BF16),
+            pltpu.VMEM((EARLY, CH, CH), BF16),
         ),
-        in_specs=[hbm_spec(), vmem_spec()],
-        out_specs=(vmem_spec(),) * 3,
+        in_specs=[hbm_spec(), vmem_spec(), hbm_spec()],
+        out_specs=(vmem_spec(),) * 4,
+        scratch_shapes=[pltpu.SemaphoreType.DMA],
         compiler_params=pltpu.CompilerParams(vmem_limit_bytes=VMEM_LIMIT),
-    )(sent, stem_weight.reshape(9, 48, CH))
+    )(sent, stem_weight.reshape(9, 48, CH), first)
 
 
 def decode(
@@ -512,27 +490,27 @@
     spread,
     stem,
     stem_bias,
+    ready,
     first,
     first_bias,
-    ready,
-    folded,
+    second,
     second_bias,
 ):
     return pl.pallas_call(
         main_kernel,
         out_shape=jax.ShapeDtypeStruct((1024, CH), BF16),
-        in_specs=[vmem_spec()] * 6
-        + [hbm_spec(), vmem_spec(), vmem_spec(), hbm_spec(), vmem_spec()],
+        in_specs=[vmem_spec()] * 7 + [hbm_spec(), vmem_spec()] * 2,
         out_specs=vmem_spec(),
         scratch_shapes=[
             pltpu.VMEM((128, 128), F32),
             pltpu.VMEM((6, 10, 16, CH), BF16),
             pltpu.VMEM((3, 6, 10, 16, CH), BF16),
             pltpu.VMEM((3, 4, 10, 16, CH), BF16),
+            pltpu.VMEM((27 - EARLY, CH, CH), BF16),
             pltpu.VMEM((3, 3, 3, CH, CH), BF16),
-            pltpu.VMEM((2, 4, 4, CH, CH), BF16),
+            pltpu.VMEM((3, 12, CH, CH), BF16),
             pltpu.VMEM((2, 1024, 128), F32),
-            pltpu.SemaphoreType.DMA((5,)),
+            pltpu.SemaphoreType.DMA((4,)),
         ],
         compiler_params=pltpu.CompilerParams(vmem_limit_bytes=VMEM_LIMIT),
     )(
@@ -542,10 +520,10 @@
         spread,
         stem,
         stem_bias[None],
+        ready,
         first,
         first_bias[None],
-        ready,
-        folded,
+        second,
         second_bias[None],
     )
 
@@ -586,17 +564,17 @@
         jnp.transpose(tile_decode_device, (2, 1, 0)),
         jnp.transpose(tile_device_slot, (2, 1, 0)),
     )
-    ready, folded = fold(upsample_second_weight)
+    first = upsample_first_weight.reshape(27, CH, CH)
     sent = pl.pallas_call(
         pick_kernel,
         out_shape=pltpu.VMEM((SEQ, 8, 128), BF16),
-        in_specs=[vmem_spec()] * 3 + [hbm_spec()],
+        in_specs=[vmem_spec()] * 3,
         out_specs=vmem_spec(),
         scratch_shapes=[pltpu.VMEM((128, 128), F32)],
         compiler_params=pltpu.CompilerParams(vmem_limit_bytes=VMEM_LIMIT),
-    )(held(own), held(other), held(pick), folded)
+    )(held(own), held(other), held(pick))
     tokens = lax.all_to_all(sent, "seq", 0, 0, tiled=True)
-    lanes, spread, stem = constants(sent, stem_conv_weight)
+    lanes, spread, stem, ready = constants(sent, stem_conv_weight, first)
     decoded = decode(
         held(tokens),
         held(place),
@@ -604,10 +582,10 @@
         held(spread),
         held(stem),
         stem_conv_bias,
-        upsample_first_weight,
+        held(ready),
+        first,
         upsample_first_bias,
-        held(ready),
-        folded,
+        upsample_second_weight,
         upsample_second_bias,
     )
     return decoded.reshape(1, 1, 2, 2, 16, 16, CH)

time: 41.8 us -> 37.7 us (0.902)
  Pallas kernels: 14.8 us -> 11.6 us
  waiting for transfers between devices: 6.1 us -> 4.9 us
    pallas_call x1 -> x0, Pallas kernels: 3.57 us -> none  [fold(): pl.pallas_call(fold_kernel, out_shape=(pltpu.VMEM((4, 4, CH, CH), BF16),...]
    pallas_call x1, Pallas kernels: 0.36 us -> 2.49 us  [constants(): pl.pallas_call(constants_kernel, out_shape=(pltpu.VMEM((512, 512), BF16),...]
    pallas_call x1, Pallas kernels: 8.62 us -> 6.93 us  [decode(): pl.pallas_call(main_kernel, out_shape=jax.ShapeDtypeStruct((1024, CH), BF...]
    all_to_all x1, waiting for transfers between devices: 6.09 us -> 4.9 us  [body(): tokens = lax.all_to_all(sent, 'seq', 0, 0, tiled=True)]
    all_to_all x1, starting transfers between devices: 8.07 us -> 8.62 us  [body(): tokens = lax.all_to_all(sent, 'seq', 0, 0, tiled=True)]
    unnamed x4 -> x2, local copies, waits for them, and re-layouts: 0.93 us -> 0.71 us
  transfers between devices with their start and end apart: 2 -> 2, of which waited for: 1 -> 1; matrix products, arithmetic and copies ran while one was open for 0% -> 0% of each run, Pallas kernels for 13% -> 10%
where the time goes in v4:
time: 37.7 us; the launch traced here: 37.4 us
  starting transfers between devices  20.1 us (53%)
  Pallas kernels  11.6 us (31%)
  waiting for transfers between devices  4.9 us (13%)
  local copies, waits for them, and re-layouts  0.71 us (2%)
    ppermute x1, starting transfers between devices, body(): lax.ppermute(own, 'req', [(i, (i + half) % requests) for i in range(reque...  11.5 us
    all_to_all x1, starting transfers between devices, body(): tokens = lax.all_to_all(sent, 'seq', 0, 0, tiled=True)  8.62 us
    pallas_call x1, Pallas kernels, decode(): pl.pallas_call(main_kernel, out_shape=jax.ShapeDtypeStruct((1024, CH), BF...  6.93 us
    all_to_all x1, waiting for transfers between devices, body(): tokens = lax.all_to_all(sent, 'seq', 0, 0, tiled=True)  4.9 us
    pallas_call x1, Pallas kernels, constants(): pl.pallas_call(constants_kernel, out_shape=(pltpu.VMEM((512, 512), BF16),...  2.49 us
    pallas_call x1, Pallas kernels, body(): pl.pallas_call(plan_kernel, out_shape=(pltpu.VMEM((256, 256), BF16), pltp...  1.35 us
    pallas_call x1, Pallas kernels, body(): pl.pallas_call(pick_kernel, out_shape=pltpu.VMEM((SEQ, 8, 128), BF16), in...  0.86 us
  transfers between devices with their start and end apart: 2, of which 1 were waited for; matrix products, arithmetic and copies ran while one was open for 0% of the time, Pallas kernels for 10%

profile of v4, /device:TPU:1, one launch (start us, length us, event | category | flops | bytes accessed | tf_op | source)
XLA Modules:
  0.0 37.4 jit_solution(9555834511752463140)
XLA Ops:
  0.0 11.5 %collective-permute-start = (bf16[64,96]{1,0:T(8,128)(2,1)}, bf16[64,96]{1,0:T(8,128)(2,1)S(1)}, u32[]{:S(2)}, u32[]{:S(2)}) collective-permute-start(bf16[64,96]{1,0:T(8,128)(2,1)} %bitcast.14), channel_id=1, source_target_pairs={{0,256},{16,272},{32,288},{48,304},{64,320},{80,336},{96,352},{112... | collective-permute-start | bytes 36872 | tf_op jit(solution)/shard_map/ppermute | solution.py:548
  11.5 1.4 %shard_map.118 = (bf16[256,256]{1,0:T(8,128)(2,1)S(1)}, bf16[448,128]{1,0:T(8,128)(2,1)S(1)}) custom-call(s32[1,32]{1,0:T(1,128)} %bitcast.24, s32[1,32]{1,0:T(1,128)} %bitcast.25, s32[1,32]{1,0:T(1,128)} %bitcast.26, s32[3,16,32]{2,1,0:T(8,128)} %bitcast.19, s32[3,16,32]{2,1,0:T(8,128)} %bitcast.20), custom_call_target="tpu_custom_call" | custom-call | tf_op jit(solution)/shard_map/pallas_call | solution.py:551
  12.8 0.0 collective-permute-done.other_ref
  12.8 0.0 copy-start
  12.8 0.7 %copy-done = bf16[1,96,1,64]{1,3,2,0:T(8,128)(2,1)S(1)} copy-done((bf16[1,96,1,64]{1,3,2,0:T(8,128)(2,1)S(1)}, bf16[1,96,1,64]{1,3,2,0:T(8,128)(2,1)}, u32[]{:S(2)}) %copy-start) | copy-done | bytes 12312
  13.6 0.9 %shard_map.119.sent_hbm = bf16[16,8,128]{2,1,0:T(8,128)(2,1)} custom-call(bf16[64,96]{1,0:T(8,128)(2,1)S(1)} %bitcast.15, bf16[64,96]{1,0:T(8,128)(2,1)S(1)} %collective-permute-done.other_ref, bf16[256,256]{1,0:T(8,128)(2,1)S(1)} %get-tuple-element.11.pick_ref), custom_call_target="tpu_custom_call" | custom-call | tf_op jit(solution)/shard_map/pallas_call | solution.py:568
  14.4 8.6 %all-to-all-start = ((bf16[16,8,128]{2,1,0:T(8,128)(2,1)}), bf16[16,8,128]{2,1,0:T(8,128)(2,1)S(1)}, u32[]{:S(2)}, u32[]{:S(2)}) async-start(bf16[16,8,128]{2,1,0:T(8,128)(2,1)} %shard_map.119.sent_hbm), calls=%async_computation | async-start | bytes 65536 | tf_op jit(solution)/shard_map/all_to_all | solution.py:576
  23.0 2.5 %shard_map.120 = (bf16[512,512]{1,0:T(8,128)(2,1)S(1)}, bf16[256,768]{1,0:T(8,128)(2,1)S(1)}, bf16[3,256,256]{2,1,0:T(8,128)(2,1)S(1)}, bf16[15,256,256]{2,1,0:T(8,128)(2,1)S(1)}) custom-call(bf16[16,8,128]{2,1,0:T(8,128)(2,1)} %shard_map.119.sent_hbm, bf16[9,48,256]{2,1,0:T(8,128)(2,1)} %bitcast.18, bf16[27,256,256]{2,1,0:T(8,128)(2,1)} %bitcast.16), custom_call_target="tpu_custom_call" | custom-call | tf_op jit(solution)/shard_map/pallas_call | solution.py:471
  25.5 4.9 %all-to-all-done.refs_0_ = bf16[16,8,128]{2,1,0:T(8,128)(2,1)S(1)} async-done(((bf16[16,8,128]{2,1,0:T(8,128)(2,1)}), bf16[16,8,128]{2,1,0:T(8,128)(2,1)S(1)}, u32[]{:S(2)}, u32[]{:S(2)}) %all-to-all-start) | async-done | bytes 32800 | tf_op jit(solution)/shard_map/all_to_all | solution.py:576
  30.4 6.9 %shard_map.121 = bf16[1024,256]{1,0:T(8,128)(2,1)} custom-call(bf16[16,8,128]{2,1,0:T(8,128)(2,1)S(1)} %all-to-all-done.refs_0_, bf16[448,128]{1,0:T(8,128)(2,1)S(1)} %get-tuple-element.12.refs_1_, bf16[512,512]{1,0:T(8,128)(2,1)S(1)} %get-tuple-element.13.refs_2_, bf16[256,768]{1,0:T(8,128)(2,1)S(1)} %get-tuple-element.14.refs_3_, ...), custom_call_target="tpu_custom_call" | custom-call | tf_op jit(solution)/shard_map/pallas_call | solution.py:499
Async XLA Ops:
  0.0 12.8 %collective-permute-start = (bf16[64,96]{1,0:T(8,128)(2,1)}, bf16[64,96]{1,0:T(8,128)(2,1)S(1)}, u32[]{:S(2)}, u32[]{:S(2)}) collective-permute-start(bf16[64,96]{1,0:T(8,128)(2,1)} %bitcast.14), channel_id=1, source_target_pairs={{0,256},{16,272},{32,288},{48,304},{64,320},{80,336},{96,352},{112... | collective-permute-start | bytes 36872 | tf_op jit(solution)/shard_map/ppermute | solution.py:548
  12.8 0.7 %copy-start = (bf16[1,96,1,64]{1,3,2,0:T(8,128)(2,1)S(1)}, bf16[1,96,1,64]{1,3,2,0:T(8,128)(2,1)}, u32[]{:S(2)}) copy-start(bf16[1,96,1,64]{1,3,2,0:T(8,128)(2,1)} %param.12) | copy-start | bytes 36868
  14.4 16.0 %all-to-all-start = ((bf16[16,8,128]{2,1,0:T(8,128)(2,1)}), bf16[16,8,128]{2,1,0:T(8,128)(2,1)S(1)}, u32[]{:S(2)}, u32[]{:S(2)}) async-start(bf16[16,8,128]{2,1,0:T(8,128)(2,1)} %shard_map.119.sent_hbm), calls=%async_computation | async-start | bytes 65536 | tf_op jit(solution)/shard_map/all_to_all | solution.py:576

commit v5 on v4

--- a/solution.py
+++ b/solution.py
@@ -31,7 +31,9 @@
     widths_ref,
     device_ref,
     slot_ref,
+    own_ref,
     pick_ref,
+    base_ref,
     place_ref,
 ):
     me = lax.axis_index("req")
@@ -95,14 +97,19 @@
             )
         )
 
-    source = iota((SEQ, 256), 1)
+    source = iota((SEQ, 128), 1)
+    mine_rows = []
     for h in range(2):
         for k in range(2):
             for pair in range(4):
                 row = (h * 8 + k * 4 + pair) * SEQ
+                wanted = codes[k] + (2 * pair + h)
+                mine_rows.append(one((source == wanted) & (source < lims[k])))
                 pick_ref[row : row + SEQ, :] = one(
-                    (source == codes[k] + (2 * pair + h)) & (source < lims[k])
+                    (source + 128 == wanted) & (source + 128 < lims[k])
                 )
+    mine_rows = jnp.concatenate(mine_rows, axis=0)
+    base_ref[...] = picked(mine_rows[:, : own_ref.shape[1]], own_ref[...])
 
     second_slot = iota((16, 128), 0) >= 8
     for n in range(4):
@@ -123,10 +130,23 @@
 
 
 def constants_kernel(
-    sent_hbm, stem_ref, first_hbm, lanes_ref, spread_ref, stem_out_ref, ready_ref, sem
+    sent_hbm,
+    stem_ref,
+    first_hbm,
+    stem_bias_ref,
+    first_bias_ref,
+    second_bias_ref,
+    lanes_ref,
+    spread_ref,
+    stem_out_ref,
+    ready_ref,
+    biases_ref,
+    sem,
 ):
     early = pltpu.make_async_copy(first_hbm.at[:EARLY], ready_ref, sem)
     early.start()
+    for n, ref in enumerate((stem_bias_ref, first_bias_ref, second_bias_ref)):
+        biases_ref[n] = jnp.broadcast_to(ref[...], (8, CH))
     row = iota((512, 512), 0)
     col = iota((512, 512), 1)
     lanes_ref[...] = one(col == (row & 3) * 128 + (row >> 6) * 16 + ((row >> 2) & 15))
@@ -148,13 +168,13 @@
     early.wait()
 
 
-def pick_kernel(own_ref, other_ref, pick_ref, out_ref, rows_ref):
-    gap = jnp.zeros((64, 32), BF16)
-    both = jnp.concatenate([own_ref[...], gap, other_ref[...], gap], axis=1)
-    picked = lax.dot_general(
-        pick_ref[...], both, (((1,), (1,)), ((), ())), preferred_element_type=F32
-    )
-    joined = jnp.concatenate([picked[:128], picked[128:]], axis=1)
+def picked(pick, tokens):
+    rows = lax.dot_general(pick, tokens, (((1,), (1,)), ((), ())), preferred_element_type=F32)
+    return jnp.concatenate([rows[:128], rows[128:]], axis=1)
+
+
+def pick_kernel(other_ref, pick_ref, base_ref, out_ref, rows_ref):
+    joined = base_ref[...] + picked(pick_ref[:, : other_ref.shape[1]], other_ref[...])
     for part in range(8):
         rows_ref[pl.ds(part, SEQ, stride=8), :] = joined[part * SEQ : (part + 1) * SEQ]
     out_ref[...] = rows_ref[...].astype(BF16).reshape(out_ref.shape)
@@ -196,13 +216,11 @@
     lanes_ref,
     spread_ref,
     stem_ref,
-    stem_bias_ref,
     ready_ref,
+    biases_ref,
     first_hbm,
-    first_bias_ref,
     second_hbm,
-    second_bias_ref,
-    out_ref,
+    out_hbm,
     rows_ref,
     taps_ref,
     one_ref,
@@ -211,6 +229,7 @@
     second_ref,
     folded_ref,
     mixed_ref,
+    stage_ref,
     sems,
     *accs,
 ):
@@ -321,7 +340,7 @@
     def finish(frame, rows, y, total, bias, ref):
         store_taps(ref, frame, y, jnp.where(rows > y, silu(total + bias), 0.0))
 
-    stem_bias = stem_bias_ref[...]
+    stem_bias = biases_ref[0, 0:1]
     multiply(
         [
             [
@@ -344,7 +363,7 @@
             for y in range(8):
                 finish(3 * m + n, rows, y, hidden[y], stem_bias, one_ref)
 
-    first_bias = first_bias_ref[...]
+    first_bias = biases_ref[1, 0:1]
     taps = [(dy, dx, dt) for dy in range(3) for dx in range(3) for dt in range(3)]
     corners = {(0, 0, 0, 0): (0, 0), (0, 1, 0, 1): (0, 2), (1, 0, 1, 0): (2, 0), (1, 1, 1, 1): (2, 2)}
     sums = [
@@ -405,7 +424,7 @@
         for y in range(8):
             finish(g, rows, y, total[y], first_bias, two_ref)
 
-    second_bias = second_bias_ref[...]
+    second_bias = biases_ref[2, 0:1]
     own_rows = [limit(start + (6 + f) < count) for f in range(2)]
     for b in range(2):
         multiply(
@@ -430,9 +449,10 @@
                 for a in range(2)
             ]
         )
-    for b in range(2):
-        for a in range(2):
-            for f in range(2):
+    sends = []
+    for f in range(2):
+        for b in range(2):
+            for a in range(2):
                 total = pltpu.matmul_pop(accs[a][2 * b + f]).reshape(8, 16, CH)
                 for y in range(8):
                     value = silu(total[y] + second_bias)
@@ -443,8 +463,15 @@
                             mixed_ref[side, pl.ds(row, 8, stride=2), :] = value[
                                 k * 8 : k * 8 + 8, side * 128 : side * 128 + 128
                             ]
-    for side in range(2):
-        out_ref[:, side * 128 : side * 128 + 128] = mixed_ref[side].astype(BF16)
+        for k in range(2):
+            rows = slice((k * 2 + f) * 256, (k * 2 + f) * 256 + 256)
+            for side in range(2):
+                stage_ref[k, f, :, side * 128 : side * 128 + 128] = mixed_ref[side, rows].astype(BF16)
+            send = pltpu.make_async_copy(stage_ref.at[k, f], out_hbm.at[k, f], sems.at[4 + 2 * f + k])
+            send.start()
+            sends.append(send)
+    for send in sends:
+        send.wait()
 
 
 def main_kernel(*refs):
@@ -467,7 +494,7 @@
     return pl.BlockSpec(memory_space=pl.ANY)
 
 
-def constants(sent, stem_weight, first):
+def constants(sent, stem_weight, first, biases):
     return pl.pallas_call(
         constants_kernel,
         out_shape=(
@@ -475,12 +502,13 @@
             pltpu.VMEM((256, 768), BF16),
             pltpu.VMEM((3, 256, CH), BF16),
             pltpu.VMEM((EARLY, CH, CH), BF16),
+            pltpu.VMEM((3, 8, CH), F32),
         ),
-        in_specs=[hbm_spec(), vmem_spec(), hbm_spec()],
-        out_specs=(vmem_spec(),) * 4,
+        in_specs=[hbm_spec(), vmem_spec(), hbm_spec()] + [vmem_spec()] * 3,
+        out_specs=(vmem_spec(),) * 5,
         scratch_shapes=[pltpu.SemaphoreType.DMA],
         compiler_params=pltpu.CompilerParams(vmem_limit_bytes=VMEM_LIMIT),
-    )(sent, stem_weight.reshape(9, 48, CH), first)
+    )(sent, stem_weight.reshape(9, 48, CH), first, *(bias[None] for bias in biases))
 
 
 def decode(
@@ -489,18 +517,16 @@
     lanes,
     spread,
     stem,
-    stem_bias,
     ready,
+    biases,
     first,
-    first_bias,
     second,
-    second_bias,
 ):
     return pl.pallas_call(
         main_kernel,
-        out_shape=jax.ShapeDtypeStruct((1024, CH), BF16),
-        in_specs=[vmem_spec()] * 7 + [hbm_spec(), vmem_spec()] * 2,
-        out_specs=vmem_spec(),
+        out_shape=jax.ShapeDtypeStruct((2, 2, 256, CH), BF16),
+        in_specs=[vmem_spec()] * 7 + [hbm_spec()] * 2,
+        out_specs=hbm_spec(),
         scratch_shapes=[
             pltpu.VMEM((128, 128), F32),
             pltpu.VMEM((6, 10, 16, CH), BF16),
@@ -510,7 +536,8 @@
             pltpu.VMEM((3, 3, 3, CH, CH), BF16),
             pltpu.VMEM((3, 12, CH, CH), BF16),
             pltpu.VMEM((2, 1024, 128), F32),
-            pltpu.SemaphoreType.DMA((4,)),
+            pltpu.VMEM((2, 2, 256, CH), BF16),
+            pltpu.SemaphoreType.DMA((8,)),
         ],
         compiler_params=pltpu.CompilerParams(vmem_limit_bytes=VMEM_LIMIT),
     )(
@@ -519,12 +546,10 @@
         lanes,
         spread,
         stem,
-        stem_bias[None],
         ready,
+        biases,
         first,
-        first_bias[None],
         second,
-        second_bias[None],
     )
 
 
@@ -548,14 +573,15 @@
     other = lax.ppermute(own, "req", [(i, (i + half) % requests) for i in range(requests)])
     shape = jax.ShapeDtypeStruct
     params = pltpu.CompilerParams(vmem_limit_bytes=60 * 1024 * 1024)
-    pick, place = pl.pallas_call(
+    pick, base, place = pl.pallas_call(
         plan_kernel,
         out_shape=(
-            pltpu.VMEM((256, 256), BF16),
+            pltpu.VMEM((256, 128), BF16),
+            pltpu.VMEM((128, 128), F32),
             pltpu.VMEM((448, 128), BF16),
         ),
-        in_specs=[vmem_spec()] * 5,
-        out_specs=(vmem_spec(),) * 2,
+        in_specs=[vmem_spec()] * 6,
+        out_specs=(vmem_spec(),) * 3,
         compiler_params=params,
     )(
         frames[None],
@@ -563,6 +589,7 @@
         widths[None],
         jnp.transpose(tile_decode_device, (2, 1, 0)),
         jnp.transpose(tile_device_slot, (2, 1, 0)),
+        own,
     )
     first = upsample_first_weight.reshape(27, CH, CH)
     sent = pl.pallas_call(
@@ -572,21 +599,21 @@
         out_specs=vmem_spec(),
         scratch_shapes=[pltpu.VMEM((128, 128), F32)],
         compiler_params=pltpu.CompilerParams(vmem_limit_bytes=VMEM_LIMIT),
-    )(held(own), held(other), held(pick))
+    )(held(other), held(pick), held(base))
     tokens = lax.all_to_all(sent, "seq", 0, 0, tiled=True)
-    lanes, spread, stem, ready = constants(sent, stem_conv_weight, first)
+    lanes, spread, stem, ready, biases = constants(
+        sent, stem_conv_weight, first, (stem_conv_bias, upsample_first_bias, upsample_second_bias)
+    )
     decoded = decode(
         held(tokens),
         held(place),
         held(lanes),
         held(spread),
         held(stem),
-        stem_conv_bias,
         held(ready),
+        held(biases),
         first,
-        upsample_first_bias,
         upsample_second_weight,
-        upsample_second_bias,
     )
     return decoded.reshape(1, 1, 2, 2, 16, 16, CH)
 

time: 37.7 us -> 36.2 us (0.960)
  local copies, waits for them, and re-layouts: 0.71 us -> 0 us
  Pallas kernels: 11.6 us -> 11.1 us
    unnamed x2 -> x0, local copies, waits for them, and re-layouts: 0.71 us -> none
    pallas_call x2, Pallas kernels: 8.28 us -> 7.71 us  [the longest x1 6.19 us: decode(): pl.pallas_call(main_kernel, out_shape=jax.ShapeDtypeStruct((2, 2, 256, CH...]
  transfers between devices with their start and end apart: 2 -> 2, of which waited for: 1 -> 1; matrix products, arithmetic and copies ran while one was open for 0% -> 0% of each run, Pallas kernels for 10% -> 11%
where the time goes in v5:
time: 36.2 us; the launch traced here: 35.9 us
  starting transfers between devices  19.9 us (55%)
  Pallas kernels  11.1 us (31%)
  waiting for transfers between devices  4.88 us (13%)
    ppermute x1, starting transfers between devices, body(): lax.ppermute(own, 'req', [(i, (i + half) % requests) for i in range(reque...  11.5 us
    all_to_all x1, starting transfers between devices, body(): tokens = lax.all_to_all(sent, 'seq', 0, 0, tiled=True)  8.45 us
    pallas_call x1, Pallas kernels, decode(): pl.pallas_call(main_kernel, out_shape=jax.ShapeDtypeStruct((2, 2, 256, CH...  6.19 us
    all_to_all x1, waiting for transfers between devices, body(): tokens = lax.all_to_all(sent, 'seq', 0, 0, tiled=True)  4.87 us
    pallas_call x1, Pallas kernels, constants(): pl.pallas_call(constants_kernel, out_shape=(pltpu.VMEM((512, 512), BF16),...  2.51 us
    pallas_call x1, Pallas kernels, body(): pl.pallas_call(plan_kernel, out_shape=(pltpu.VMEM((256, 128), BF16), pltp...  1.52 us
    pallas_call x1, Pallas kernels, body(): pl.pallas_call(pick_kernel, out_shape=pltpu.VMEM((SEQ, 8, 128), BF16), in...  0.85 us
  transfers between devices with their start and end apart: 2, of which 1 were waited for; matrix products, arithmetic and copies ran while one was open for 0% of the time, Pallas kernels for 11%

profile of v5, /device:TPU:1, one launch (start us, length us, event | category | flops | bytes accessed | tf_op | source)
XLA Modules:
  0.0 35.9 jit_solution(18268316537633931728)
XLA Ops:
  0.0 11.5 %collective-permute-start = (bf16[64,96]{1,0:T(8,128)(2,1)}, bf16[64,96]{1,0:T(8,128)(2,1)S(1)}, u32[]{:S(2)}, u32[]{:S(2)}) collective-permute-start(bf16[64,96]{1,0:T(8,128)(2,1)} %bitcast.19), channel_id=1, source_target_pairs={{0,256},{16,272},{32,288},{48,304},{64,320},{80,336},{96,352},{112... | collective-permute-start | bytes 36872 | tf_op jit(solution)/shard_map/ppermute | solution.py:573
  11.5 1.5 %shard_map.118 = (bf16[256,128]{1,0:T(8,128)(2,1)S(1)}, f32[128,128]{1,0:T(8,128)S(1)}, bf16[448,128]{1,0:T(8,128)(2,1)S(1)}) custom-call(s32[1,32]{1,0:T(1,128)} %bitcast.24, s32[1,32]{1,0:T(1,128)} %bitcast.25, s32[1,32]{1,0:T(1,128)} %bitcast.26, s32[3,16,32]{2,1,0:T(8,128)} %bitcast.17, s32[3,16,32]{2,1,0:T(8,128)} %bitcast.18, bf16[64,96]{1,0:T(8,128)(2,1)} %bitcast.20), custom_call_target="tpu_custom_call" | custom-call | tf_op jit(solution)/shard_map/pallas_call | solution.py:576
  13.0 0.0 collective-permute-done.other_ref
  13.0 0.8 %shard_map.119.sent_hbm = bf16[16,8,128]{2,1,0:T(8,128)(2,1)} custom-call(bf16[64,96]{1,0:T(8,128)(2,1)S(1)} %collective-permute-done.other_ref, bf16[256,128]{1,0:T(8,128)(2,1)S(1)} %get-tuple-element.13.pick_ref, f32[128,128]{1,0:T(8,128)S(1)} %get-tuple-element.14.base_ref), custom_call_target="tpu_custom_call" | custom-call | tf_op jit(solution)/shard_map/pallas_call | solution.py:595
  13.9 8.4 %all-to-all-start = ((bf16[16,8,128]{2,1,0:T(8,128)(2,1)}), bf16[16,8,128]{2,1,0:T(8,128)(2,1)S(1)}, u32[]{:S(2)}, u32[]{:S(2)}) async-start(bf16[16,8,128]{2,1,0:T(8,128)(2,1)} %shard_map.119.sent_hbm), calls=%async_computation | async-start | bytes 65536 | tf_op jit(solution)/shard_map/all_to_all | solution.py:603
  22.3 2.5 %shard_map.120 = (bf16[512,512]{1,0:T(8,128)(2,1)S(1)}, bf16[256,768]{1,0:T(8,128)(2,1)S(1)}, bf16[3,256,256]{2,1,0:T(8,128)(2,1)S(1)}, bf16[15,256,256]{2,1,0:T(8,128)(2,1)S(1)}, f32[3,8,256]{2,1,0:T(8,128)S(1)}) custom-call(bf16[16,8,128]{2,1,0:T(8,128)(2,1)} %shard_map.119.sent_hbm, bf16[9,48,256]{2,1,0:T(8,128)(2,1)} %bitcast.16, ...), custom_call_target="tpu_custom_call" | custom-call | tf_op jit(solution)/shard_map/pallas_call | solution.py:498
  24.8 4.9 %all-to-all-done.refs_0_ = bf16[16,8,128]{2,1,0:T(8,128)(2,1)S(1)} async-done(((bf16[16,8,128]{2,1,0:T(8,128)(2,1)}), bf16[16,8,128]{2,1,0:T(8,128)(2,1)S(1)}, u32[]{:S(2)}, u32[]{:S(2)}) %all-to-all-start) | async-done | bytes 32800 | tf_op jit(solution)/shard_map/all_to_all | solution.py:603
  29.7 6.2 %shard_map.121 = bf16[2,2,256,256]{3,2,1,0:T(8,128)(2,1)} custom-call(bf16[16,8,128]{2,1,0:T(8,128)(2,1)S(1)} %all-to-all-done.refs_0_, bf16[448,128]{1,0:T(8,128)(2,1)S(1)} %get-tuple-element.15.refs_1_, bf16[512,512]{1,0:T(8,128)(2,1)S(1)} %get-tuple-element.16.refs_2_, bf16[256,768]{1,0:T(8,128)(2,1)S(1)} %get-tuple-element.17.refs_3_, ...), custom_call_target="tpu_custom_call" | custom-call | tf_op jit(solution)/shard_map/pallas_call | solution.py:525
Async XLA Ops:
  0.0 13.0 %collective-permute-start = (bf16[64,96]{1,0:T(8,128)(2,1)}, bf16[64,96]{1,0:T(8,128)(2,1)S(1)}, u32[]{:S(2)}, u32[]{:S(2)}) collective-permute-start(bf16[64,96]{1,0:T(8,128)(2,1)} %bitcast.19), channel_id=1, source_target_pairs={{0,256},{16,272},{32,288},{48,304},{64,320},{80,336},{96,352},{112... | collective-permute-start | bytes 36872 | tf_op jit(solution)/shard_map/ppermute | solution.py:573
  13.9 15.8 %all-to-all-start = ((bf16[16,8,128]{2,1,0:T(8,128)(2,1)}), bf16[16,8,128]{2,1,0:T(8,128)(2,1)S(1)}, u32[]{:S(2)}, u32[]{:S(2)}) async-start(bf16[16,8,128]{2,1,0:T(8,128)(2,1)} %shard_map.119.sent_hbm), calls=%async_computation | async-start | bytes 65536 | tf_op jit(solution)/shard_map/all_to_all | solution.py:603

commit v6 on v5

--- a/solution.py
+++ b/solution.py
@@ -35,6 +35,7 @@
     pick_ref,
     base_ref,
     place_ref,
+    rows_ref,
 ):
     me = lax.axis_index("req")
     column = lax.axis_index("seq")
@@ -98,18 +99,17 @@
         )
 
     source = iota((SEQ, 128), 1)
-    mine_rows = []
     for h in range(2):
         for k in range(2):
             for pair in range(4):
-                row = (h * 8 + k * 4 + pair) * SEQ
                 wanted = codes[k] + (2 * pair + h)
-                mine_rows.append(one((source == wanted) & (source < lims[k])))
-                pick_ref[row : row + SEQ, :] = one(
-                    (source + 128 == wanted) & (source + 128 < lims[k])
-                )
-    mine_rows = jnp.concatenate(mine_rows, axis=0)
-    base_ref[...] = picked(mine_rows[:, : own_ref.shape[1]], own_ref[...])
+                rows = pl.ds(h * 128 + k * 4 + pair, SEQ, stride=8)
+                mine = (source == wanted) & (source < lims[k])
+                theirs = (source + 128 == wanted) & (source + 128 < lims[k])
+                rows_ref[0, rows, :] = jnp.where(mine, 1.0, 0.0)
+                rows_ref[1, rows, :] = jnp.where(theirs, 1.0, 0.0)
+    pick_ref[...] = rows_ref[1].astype(BF16)
+    base_ref[...] = picked(rows_ref[0, :, : own_ref.shape[1]].astype(BF16), own_ref[...])
 
     second_slot = iota((16, 128), 0) >= 8
     for n in range(4):
@@ -173,11 +173,9 @@
     return jnp.concatenate([rows[:128], rows[128:]], axis=1)
 
 
-def pick_kernel(other_ref, pick_ref, base_ref, out_ref, rows_ref):
+def pick_kernel(other_ref, pick_ref, base_ref, out_ref):
     joined = base_ref[...] + picked(pick_ref[:, : other_ref.shape[1]], other_ref[...])
-    for part in range(8):
-        rows_ref[pl.ds(part, SEQ, stride=8), :] = joined[part * SEQ : (part + 1) * SEQ]
-    out_ref[...] = rows_ref[...].astype(BF16).reshape(out_ref.shape)
+    out_ref[...] = joined.astype(BF16).reshape(out_ref.shape)
 
 
 def silu(v):
@@ -426,43 +424,50 @@
 
     second_bias = biases_ref[2, 0:1]
     own_rows = [limit(start + (6 + f) < count) for f in range(2)]
-    for b in range(2):
-        multiply(
+    def second_step(t, a, b, ty, tx):
+        return (
+            lambda: weights_of(t, a, b, ty, tx),
             [
-                [
-                    (
-                        lambda a=a, b=b, ty=ty, tx=tx, dt=dt: weights_of(dt, a, b, ty, tx),
-                        [
-                            (
-                                accs[a][2 * b + f],
-                                lambda f=f, a=a, b=b, ty=ty, tx=tx, dt=dt: two_ref[
-                                    b + tx, dt + f, a + ty : a + ty + 8
-                                ].reshape(128, CH),
-                            )
-                            for f in range(2)
-                        ],
-                    )
-                    for ty in range(2)
-                    for tx in range(2)
-                    for dt in range(3)
-                ]
-                for a in range(2)
-            ]
+                (
+                    accs[a][2 * b + f],
+                    lambda f=f: two_ref[b + tx, t + f, a + ty : a + ty + 8].reshape(128, CH),
+                )
+                for f in range(2)
+            ],
         )
+
+    values = {}
+
+    def second_rows(a, b, f, rows):
+        if (a, b, f) not in values:
+            values[a, b, f] = pltpu.matmul_pop(accs[a][2 * b + f]).reshape(8, 16, CH)
+        for y in rows:
+            value = silu(values[a, b, f][y] + second_bias)
+            value = jnp.where(own_rows[f] > y, value, 0.0)
+            for k in range(2):
+                row = ((k * 2 + f) * 16 + 2 * y + a) * 16 + b
+                for side in range(2):
+                    mixed_ref[side, pl.ds(row, 8, stride=2), :] = value[
+                        k * 8 : k * 8 + 8, side * 128 : side * 128 + 128
+                    ]
+
+    taps = [(ty, tx) for ty in range(2) for tx in range(2)]
+    multiply(
+        [
+            [second_step(t, a, b, *tap) for b in range(2) for t in range(3) for tap in taps]
+            for a in range(2)
+        ],
+        [
+            (14 + (f * 2 + a) * 2 + part, functools.partial(second_rows, a, 0, f, range(part * 4, part * 4 + 4)))
+            for f in range(2)
+            for a in range(2)
+            for part in range(2)
+        ],
+    )
     sends = []
     for f in range(2):
-        for b in range(2):
-            for a in range(2):
-                total = pltpu.matmul_pop(accs[a][2 * b + f]).reshape(8, 16, CH)
-                for y in range(8):
-                    value = silu(total[y] + second_bias)
-                    value = jnp.where(own_rows[f] > y, value, 0.0)
-                    for k in range(2):
-                        row = ((k * 2 + f) * 16 + 2 * y + a) * 16 + b
-                        for side in range(2):
-                            mixed_ref[side, pl.ds(row, 8, stride=2), :] = value[
-                                k * 8 : k * 8 + 8, side * 128 : side * 128 + 128
-                            ]
+        for a in range(2):
+            second_rows(a, 1, f, range(8))
         for k in range(2):
             rows = slice((k * 2 + f) * 256, (k * 2 + f) * 256 + 256)
             for side in range(2):
@@ -582,6 +587,7 @@
         ),
         in_specs=[vmem_spec()] * 6,
         out_specs=(vmem_spec(),) * 3,
+        scratch_shapes=[pltpu.VMEM((2, 256, 128), F32)],
         compiler_params=params,
     )(
         frames[None],
@@ -597,7 +603,6 @@
         out_shape=pltpu.VMEM((SEQ, 8, 128), BF16),
         in_specs=[vmem_spec()] * 3,
         out_specs=vmem_spec(),
-        scratch_shapes=[pltpu.VMEM((128, 128), F32)],
         compiler_params=pltpu.CompilerParams(vmem_limit_bytes=VMEM_LIMIT),
     )(held(other), held(pick), held(base))
     tokens = lax.all_to_all(sent, "seq", 0, 0, tiled=True)

time: 36.2 us -> 36.1 us (level)
  no operation moved by 1% of the time
where the time goes in v6:
time: 36.1 us; the launch traced here: 35.8 us
  starting transfers between devices  19.9 us (55%)
  Pallas kernels  11 us (30%)
  waiting for transfers between devices  4.88 us (14%)
    ppermute x1, starting transfers between devices, body(): lax.ppermute(own, 'req', [(i, (i + half) % requests) for i in range(reque...  11.5 us
    all_to_all x1, starting transfers between devices, body(): tokens = lax.all_to_all(sent, 'seq', 0, 0, tiled=True)  8.47 us
    pallas_call x1, Pallas kernels, decode(): pl.pallas_call(main_kernel, out_shape=jax.ShapeDtypeStruct((2, 2, 256, CH...  6.12 us
    all_to_all x1, waiting for transfers between devices, body(): tokens = lax.all_to_all(sent, 'seq', 0, 0, tiled=True)  4.87 us
    pallas_call x1, Pallas kernels, constants(): pl.pallas_call(constants_kernel, out_shape=(pltpu.VMEM((512, 512), BF16),...  2.51 us
    pallas_call x1, Pallas kernels, body(): pl.pallas_call(plan_kernel, out_shape=(pltpu.VMEM((256, 128), BF16), pltp...  1.5 us
    pallas_call x1, Pallas kernels, body(): pl.pallas_call(pick_kernel, out_shape=pltpu.VMEM((SEQ, 8, 128), BF16), in...  0.83 us
  transfers between devices with their start and end apart: 2, of which 1 were waited for; matrix products, arithmetic and copies ran while one was open for 0% of the time, Pallas kernels for 11%

profile of v6, /device:TPU:1, one launch (start us, length us, event | category | flops | bytes accessed | tf_op | source)
XLA Modules:
  0.0 35.8 jit_solution(12478822257306961080)
XLA Ops:
  0.0 11.5 %collective-permute-start = (bf16[64,96]{1,0:T(8,128)(2,1)}, bf16[64,96]{1,0:T(8,128)(2,1)S(1)}, u32[]{:S(2)}, u32[]{:S(2)}) collective-permute-start(bf16[64,96]{1,0:T(8,128)(2,1)} %bitcast.19), channel_id=1, source_target_pairs={{0,256},{16,272},{32,288},{48,304},{64,320},{80,336},{96,352},{112... | collective-permute-start | bytes 36872 | tf_op jit(solution)/shard_map/ppermute | solution.py:578
  11.5 1.5 %shard_map.118 = (bf16[256,128]{1,0:T(8,128)(2,1)S(1)}, f32[128,128]{1,0:T(8,128)S(1)}, bf16[448,128]{1,0:T(8,128)(2,1)S(1)}) custom-call(s32[1,32]{1,0:T(1,128)} %bitcast.24, s32[1,32]{1,0:T(1,128)} %bitcast.25, s32[1,32]{1,0:T(1,128)} %bitcast.26, s32[3,16,32]{2,1,0:T(8,128)} %bitcast.17, s32[3,16,32]{2,1,0:T(8,128)} %bitcast.18, bf16[64,96]{1,0:T(8,128)(2,1)} %bitcast.20), custom_call_target="tpu_custom_call" | custom-call | tf_op jit(solution)/shard_map/pallas_call | solution.py:581
  13.0 0.0 collective-permute-done.other_ref
  13.0 0.8 %shard_map.119.sent_hbm = bf16[16,8,128]{2,1,0:T(8,128)(2,1)} custom-call(bf16[64,96]{1,0:T(8,128)(2,1)S(1)} %collective-permute-done.other_ref, bf16[256,128]{1,0:T(8,128)(2,1)S(1)} %get-tuple-element.13.pick_ref, f32[128,128]{1,0:T(8,128)S(1)} %get-tuple-element.14.base_ref), custom_call_target="tpu_custom_call" | custom-call | tf_op jit(solution)/shard_map/pallas_call | solution.py:601
  13.8 8.5 %all-to-all-start = ((bf16[16,8,128]{2,1,0:T(8,128)(2,1)}), bf16[16,8,128]{2,1,0:T(8,128)(2,1)S(1)}, u32[]{:S(2)}, u32[]{:S(2)}) async-start(bf16[16,8,128]{2,1,0:T(8,128)(2,1)} %shard_map.119.sent_hbm), calls=%async_computation | async-start | bytes 65536 | tf_op jit(solution)/shard_map/all_to_all | solution.py:608
  22.3 2.5 %shard_map.120 = (bf16[512,512]{1,0:T(8,128)(2,1)S(1)}, bf16[256,768]{1,0:T(8,128)(2,1)S(1)}, bf16[3,256,256]{2,1,0:T(8,128)(2,1)S(1)}, bf16[15,256,256]{2,1,0:T(8,128)(2,1)S(1)}, f32[3,8,256]{2,1,0:T(8,128)S(1)}) custom-call(bf16[16,8,128]{2,1,0:T(8,128)(2,1)} %shard_map.119.sent_hbm, bf16[9,48,256]{2,1,0:T(8,128)(2,1)} %bitcast.16, ...), custom_call_target="tpu_custom_call" | custom-call | tf_op jit(solution)/shard_map/pallas_call | solution.py:503
  24.8 4.9 %all-to-all-done.refs_0_ = bf16[16,8,128]{2,1,0:T(8,128)(2,1)S(1)} async-done(((bf16[16,8,128]{2,1,0:T(8,128)(2,1)}), bf16[16,8,128]{2,1,0:T(8,128)(2,1)S(1)}, u32[]{:S(2)}, u32[]{:S(2)}) %all-to-all-start) | async-done | bytes 32800 | tf_op jit(solution)/shard_map/all_to_all | solution.py:608
  29.7 6.1 %shard_map.121 = bf16[2,2,256,256]{3,2,1,0:T(8,128)(2,1)} custom-call(bf16[16,8,128]{2,1,0:T(8,128)(2,1)S(1)} %all-to-all-done.refs_0_, bf16[448,128]{1,0:T(8,128)(2,1)S(1)} %get-tuple-element.15.refs_1_, bf16[512,512]{1,0:T(8,128)(2,1)S(1)} %get-tuple-element.16.refs_2_, bf16[256,768]{1,0:T(8,128)(2,1)S(1)} %get-tuple-element.17.refs_3_, ...), custom_call_target="tpu_custom_call" | custom-call | tf_op jit(solution)/shard_map/pallas_call | solution.py:530
Async XLA Ops:
  0.0 13.0 %collective-permute-start = (bf16[64,96]{1,0:T(8,128)(2,1)}, bf16[64,96]{1,0:T(8,128)(2,1)S(1)}, u32[]{:S(2)}, u32[]{:S(2)}) collective-permute-start(bf16[64,96]{1,0:T(8,128)(2,1)} %bitcast.19), channel_id=1, source_target_pairs={{0,256},{16,272},{32,288},{48,304},{64,320},{80,336},{96,352},{112... | collective-permute-start | bytes 36872 | tf_op jit(solution)/shard_map/ppermute | solution.py:578
  13.8 15.9 %all-to-all-start = ((bf16[16,8,128]{2,1,0:T(8,128)(2,1)}), bf16[16,8,128]{2,1,0:T(8,128)(2,1)S(1)}, u32[]{:S(2)}, u32[]{:S(2)}) async-start(bf16[16,8,128]{2,1,0:T(8,128)(2,1)} %shard_map.119.sent_hbm), calls=%async_computation | async-start | bytes 65536 | tf_op jit(solution)/shard_map/all_to_all | solution.py:608
